TPU v7x, 128 devices: a whole 4x4x4 slice. The times are simulated.
128 devices in a mesh: dp: 4 (over x_hi, core), feat: 32 (over y, z, x_lo).
Axes of the slice: x: 4 (x_hi: 2, x_lo: 2; x = x_hi * 2 + x_lo), y: 4, z: 4, core: 2. Of those that a mesh axis runs over, the one named last changes fastest.
Arguments:
- tokens: bfloat16 [4096, 16384], P('dp', 'feat'), may hold values from -6 to 6
- butterfly: bfloat16 [16384, 3072], P('feat'), may hold values from -0.109375 to 0.109375
- left_factor: bfloat16 [16384, 256], P('feat'), may hold values from -0.046875 to 0.046875
- right_factor: bfloat16 [256, 16384], P(None, 'feat'), may hold values from -0.375 to 0.375
- cotangent: bfloat16 [4096, 16384], P('dp', 'feat'), may hold values from -6 to 6
Outputs:
- output: bfloat16 [4096, 16384], P('dp', 'feat')
- grad_tokens: bfloat16 [4096, 16384], P('dp', 'feat')
- grad_butterfly: float32 [16384, 3072], P('feat')
- grad_left: float32 [16384, 256], P('feat')
- grad_right: float32 [256, 16384], P(None, 'feat')
All inputs are finite; a program needn't handle non-finite values.
Results may differ from a plain program's by a relative error of at most 0.0057.
Values may be sent and summed in bfloat16 or wider, within the bound.
No kernel may reach another device: no remote copies, remote signals or barrier semaphores. Data moves between devices by JAX's collectives and lax.ppermute only.
A program may use at most 128 MiB of HBM per device.

v0:
```python
import jax
import jax.numpy as jnp
from jax import lax
from jax.sharding import PartitionSpec as P


def from_partner(block, axis, distance):
    count = lax.axis_size(axis)
    route = []
    for low in range(count):
        high = low | 1 << distance
        if high != low and high < count:
            route += [(low, high), (high, low)]
    return lax.ppermute(block, axis, route)


def normal_cdf(value):
    return 0.5 * (1.0 + lax.erf(value * 0.7071067811865476))


def contract(first, second, first_dim, second_dim):
    return lax.dot_general(
        first, second, (((first_dim,), (second_dim,)), ((), ())), preferred_element_type=jnp.float32
    )


def shards(tokens, butterfly, left_factor, right_factor, cotangent):
    levels = lax.axis_size("feat").bit_length() - 1
    block_size = tokens.shape[1]

    def weight_block(slot):
        return butterfly[:, slot * block_size : (slot + 1) * block_size]

    partners = []
    for level in range(levels):
        partners.append(from_partner(tokens, "feat", level))
    local_low = jnp.dot(tokens, left_factor, preferred_element_type=jnp.float32)
    reduced = lax.psum(local_low, "feat").astype(jnp.bfloat16)
    pre = jnp.dot(tokens, weight_block(0), preferred_element_type=jnp.float32)
    pre = pre + jnp.dot(reduced, right_factor, preferred_element_type=jnp.float32)
    for level in range(levels):
        pre = pre + jnp.dot(
            partners[level], weight_block(level + 1), preferred_element_type=jnp.float32
        )
    output = (pre * normal_cdf(pre)).astype(jnp.bfloat16)
    density = jnp.exp(-0.5 * pre * pre) * 0.3989422804014327
    delta = (cotangent.astype(jnp.float32) * (normal_cdf(pre) + pre * density)).astype(jnp.bfloat16)
    grad_parts = [contract(tokens, delta, 0, 0)]
    for level in range(levels):
        grad_parts.append(contract(partners[level], delta, 0, 0))
    grad_blocks = jnp.concatenate(grad_parts, axis=1)
    grad_right_local = contract(reduced, delta, 0, 0)
    local_back = contract(delta, right_factor, 1, 1)
    back_reduced = lax.psum(local_back, "feat").astype(jnp.bfloat16)
    grad_left_local = contract(tokens, back_reduced, 0, 0)
    back = contract(delta, weight_block(0), 1, 1) + contract(back_reduced, left_factor, 1, 1)
    for level in range(levels):
        back = back + from_partner(contract(delta, weight_block(level + 1), 1, 1), "feat", level)
    grad_butterfly, grad_left, grad_right = lax.psum(
        (grad_blocks, grad_left_local, grad_right_local), "dp"
    )
    return (output, back.astype(jnp.bfloat16), grad_butterfly, grad_left, grad_right)


def solution(mesh):
    in_specs = (P("dp", "feat"), P("feat", None), P("feat", None), P(None, "feat"), P("dp", "feat"))
    out_specs = (
        P("dp", "feat"),
        P("dp", "feat"),
        P("feat", None),
        P("feat", None),
        P(None, "feat"),
    )
    return jax.shard_map(shards, mesh=mesh, in_specs=in_specs, out_specs=out_specs, check_vma=False)
```

profile of v0, /device:TPU:1, one launch (start us, length us, event | category | flops | bytes accessed | tf_op | source)
XLA Modules:
  0.0 597.9 jit_solution(3866572160524782804)
XLA Ops:
  7.2 3.8 collective-permute-start.4
  11.5 3.6 collective-permute-start.2
  18.7 161.5 %all-reduce.6 = bf16[1024,256]{1,0:T(8,128)(2,1)S(1)} all-reduce(f32[1024,256]{1,0:T(8,128)S(1)} %fusion.44), channel_id=1, replica_groups=mesh['dp'=4,'feat'=32] {'feat'}, use_global_device_ids=true, to_apply=%region_0.0 | all-reduce | flops 262144 | bytes 1572864 | tf_op jit(solution)/shard_map/psum | solution.py:38
  180.3 1.9 fusion.36
  182.6 1.9 fusion.20
  184.6 1.9 fusion.24
  186.5 1.9 fusion.28
  188.5 2.0 fusion.32
  190.5 4.0 fusion.5
  198.9 143.5 %all-reduce.7 = bf16[1024,256]{1,0:T(8,128)(2,1)S(1)} all-reduce(f32[1024,256]{1,0:T(8,128)} %fusion.45), channel_id=1, replica_groups=mesh['dp'=4,'feat'=32] {'feat'}, use_global_device_ids=true, to_apply=%region_1.0 | all-reduce | flops 262144 | bytes 1572864 | tf_op jit(solution)/shard_map/psum | solution.py:54
  343.7 2.9 fusion.10
  346.7 2.9 fusion.9
  349.6 2.9 fusion.8
  352.5 2.9 fusion.7
  355.4 2.9 fusion.6
  358.4 1.9 fusion.12
  363.7 1.7 collective-permute-start.6
  365.4 2.6 collective-permute-start.5
  368.8 21.1 %collective-permute-done.9 = f32[1024,512]{1,0:T(8,128)S(1)} collective-permute-done((f32[1024,512]{1,0:T(8,128)S(1)}, f32[1024,512]{1,0:T(8,128)S(1)}, u32[]{:S(2)}, u32[]{:S(2)}) %collective-permute-start.9) | collective-permute-done | bytes 2097184 | tf_op jit(solution)/shard_map/ppermute | solution.py:14
  389.9 19.1 %collective-permute-done.8 = f32[1024,512]{1,0:T(8,128)S(1)} collective-permute-done((f32[1024,512]{1,0:T(8,128)S(1)}, f32[1024,512]{1,0:T(8,128)S(1)}, u32[]{:S(2)}, u32[]{:S(2)}) %collective-permute-start.8) | collective-permute-done | bytes 2097184 | tf_op jit(solution)/shard_map/ppermute | solution.py:14
  409.0 3.4 collective-permute-done.6
  412.4 1.8 add_convert_fusion
  414.1 168.5 %all-reduce.5.cloned.1.call-done = (f32[512,3072]{0,1:T(8,128)}, f32[512,256]{0,1:T(8,128)}, f32[256,512]{1,0:T(8,128)}) async-done(((f32[512,3072]{0,1:T(8,128)}, f32[512,256]{0,1:T(8,128)}, f32[256,512]{1,0:T(8,128)}), (f32[512,3072]{0,1:T(8,128)}, f32[512,256]{0,1:T(8,128)}, f32[256,512]{1,0:T(8,128)})) %all-reduce.5.cloned.1.call-update) | async-done | bytes 7340048 | tf_op jit(solution)/shard_map/psum | solution.py:59
  582.6 6.7 %copy.10 = f32[512,3072]{1,0:T(8,128)} copy(f32[512,3072]{0,1:T(8,128)} %get-tuple-element.10) | data formatting | bytes 12582912
  (46 shorter events, 16.1 us)
Async XLA Ops:
  7.2 175.0 %copy-start = (bf16[256,512]{1,0:T(8,128)(2,1)S(1)}, bf16[256,512]{1,0:T(8,128)(2,1)}, u32[]{:S(2)}) copy-start(bf16[256,512]{1,0:T(8,128)(2,1)} %param.8) | copy-start | bytes 786436
  7.2 173.1 %copy-start.4 = (bf16[1024,512]{1,0:T(8,128)(2,1)S(1)}, bf16[1024,512]{1,0:T(8,128)(2,1)}, u32[]{:S(2)}) copy-start(bf16[1024,512]{1,0:T(8,128)(2,1)} %param.5) | copy-start | bytes 3145732
  7.2 575.4 %all-reduce.5.cloned.1.call-start = ((), (), s32[]{:S(2)}) async-start(), calls=%async_computation | async-start | bytes 14680064 | tf_op jit(solution)/shard_map/psum | solution.py:59
  7.2 183.3 %collective-permute-start.4 = (bf16[1024,512]{1,0:T(8,128)(2,1)}, bf16[1024,512]{1,0:T(8,128)(2,1)}, u32[]{:S(2)}, u32[]{:S(2)}) collective-permute-start(bf16[1024,512]{1,0:T(8,128)(2,1)} %param.5), channel_id=1, source_target_pairs={{0,16},{16,0},{1,17},{17,1},{2,18},{18,2},{3,19},{19,3},{4,20},{20... | collective-permute-start | bytes 3145736 | tf_op jit(solution)/shard_map/ppermute | solution.py:14
  11.1 171.5 %collective-permute-start.3 = (bf16[1024,512]{1,0:T(8,128)(2,1)}, bf16[1024,512]{1,0:T(8,128)(2,1)}, u32[]{:S(2)}, u32[]{:S(2)}) collective-permute-start(bf16[1024,512]{1,0:T(8,128)(2,1)} %param.5), channel_id=1, source_target_pairs={{0,8},{8,0},{1,9},{9,1},{2,10},{10,2},{3,11},{11,3},{4,12},{12,4},... | collective-permute-start | bytes 3145736 | tf_op jit(solution)/shard_map/ppermute | solution.py:14
  11.5 173.1 %collective-permute-start.2 = (bf16[1024,512]{1,0:T(8,128)(2,1)}, bf16[1024,512]{1,0:T(8,128)(2,1)}, u32[]{:S(2)}, u32[]{:S(2)}) collective-permute-start(bf16[1024,512]{1,0:T(8,128)(2,1)} %param.5), channel_id=1, source_target_pairs={{0,4},{4,0},{1,5},{5,1},{2,6},{6,2},{3,7},{7,3},{8,12},{12,8},{9,1... | collective-permute-start | bytes 3145736 | tf_op jit(solution)/shard_map/ppermute | solution.py:14
  15.1 171.5 %collective-permute-start.1 = (bf16[1024,512]{1,0:T(8,128)(2,1)}, bf16[1024,512]{1,0:T(8,128)(2,1)}, u32[]{:S(2)}, u32[]{:S(2)}) collective-permute-start(bf16[1024,512]{1,0:T(8,128)(2,1)} %param.5), channel_id=1, source_target_pairs={{0,2},{2,0},{1,3},{3,1},{4,6},{6,4},{5,7},{7,5},{8,10},{10,8},{9,1... | collective-permute-start | bytes 3145736 | tf_op jit(solution)/shard_map/ppermute | solution.py:14
  15.8 172.7 %collective-permute-start = (bf16[1024,512]{1,0:T(8,128)(2,1)}, bf16[1024,512]{1,0:T(8,128)(2,1)}, u32[]{:S(2)}, u32[]{:S(2)}) collective-permute-start(bf16[1024,512]{1,0:T(8,128)(2,1)} %param.5), channel_id=1, source_target_pairs={{0,1},{1,0},{2,3},{3,2},{4,5},{5,4},{6,7},{7,6},{8,9},{9,8},{10,11... | collective-permute-start | bytes 3145736 | tf_op jit(solution)/shard_map/ppermute | solution.py:14
  180.3 2.4 copy-start.2
  188.5 2.1 copy-start.6
  358.4 2.1 copy-start.3
  363.4 48.9 %copy-start.5 = (bf16[512,256]{1,0:T(8,128)(2,1)S(1)}, bf16[512,256]{1,0:T(8,128)(2,1)}, u32[]{:S(2)}) copy-start(bf16[512,256]{1,0:T(8,128)(2,1)} %param.7) | copy-start | bytes 786436
  363.4 26.5 %collective-permute-start.9 = (f32[1024,512]{1,0:T(8,128)S(1)}, f32[1024,512]{1,0:T(8,128)S(1)}, u32[]{:S(2)}, u32[]{:S(2)}) collective-permute-start(f32[1024,512]{1,0:T(8,128)S(1)} %fusion.12), channel_id=1, source_target_pairs={{0,16},{16,0},{1,17},{17,1},{2,18},{18,2},{3,19},{19,3},{4,20},{20... | collective-permute-start | bytes 6291464 | tf_op jit(solution)/shard_map/ppermute | solution.py:14
  363.5 45.4 %collective-permute-start.8 = (f32[1024,512]{1,0:T(8,128)S(1)}, f32[1024,512]{1,0:T(8,128)S(1)}, u32[]{:S(2)}, u32[]{:S(2)}) collective-permute-start(f32[1024,512]{1,0:T(8,128)S(1)} %fusion.18), channel_id=1, source_target_pairs={{0,8},{8,0},{1,9},{9,1},{2,10},{10,2},{3,11},{11,3},{4,12},{12,4},... | collective-permute-start | bytes 6291464 | tf_op jit(solution)/shard_map/ppermute | solution.py:14
  363.6 45.4 %collective-permute-start.7 = (f32[1024,512]{1,0:T(8,128)S(1)}, f32[1024,512]{1,0:T(8,128)S(1)}, u32[]{:S(2)}, u32[]{:S(2)}) collective-permute-start(f32[1024,512]{1,0:T(8,128)S(1)} %fusion.22), channel_id=1, source_target_pairs={{0,4},{4,0},{1,5},{5,1},{2,6},{6,2},{3,7},{7,3},{8,12},{12,8},{9,1... | collective-permute-start | bytes 6291464 | tf_op jit(solution)/shard_map/ppermute | solution.py:14
  363.7 48.6 %collective-permute-start.6 = (f32[1024,512]{1,0:T(8,128)S(1)}, f32[1024,512]{1,0:T(8,128)S(1)}, u32[]{:S(2)}, u32[]{:S(2)}) collective-permute-start(f32[1024,512]{1,0:T(8,128)S(1)} %fusion.26), channel_id=1, source_target_pairs={{0,2},{2,0},{1,3},{3,1},{4,6},{6,4},{5,7},{7,5},{8,10},{10,8},{9,1... | collective-permute-start | bytes 6291464 | tf_op jit(solution)/shard_map/ppermute | solution.py:14
  365.4 46.9 %collective-permute-start.5 = (f32[1024,512]{1,0:T(8,128)S(1)}, f32[1024,512]{1,0:T(8,128)S(1)}, u32[]{:S(2)}, u32[]{:S(2)}) collective-permute-start(f32[1024,512]{1,0:T(8,128)S(1)} %fusion.30), channel_id=1, source_target_pairs={{0,1},{1,0},{2,3},{3,2},{4,5},{5,4},{6,7},{7,6},{8,9},{9,8},{10,11... | collective-permute-start | bytes 6291464 | tf_op jit(solution)/shard_map/ppermute | solution.py:14
  582.6 6.7 %copy-start.8 = (f32[512,256]{0,1:T(8,128)S(1)}, f32[512,256]{0,1:T(8,128)}, u32[]{:S(2)}) copy-start(f32[512,256]{0,1:T(8,128)} %get-tuple-element.11) | copy-start | bytes 1572868
  582.6 7.7 %copy-start.7 = (f32[256,512]{1,0:T(8,128)S(1)}, f32[256,512]{1,0:T(8,128)}, u32[]{:S(2)}) copy-start(f32[256,512]{1,0:T(8,128)} %get-tuple-element.19) | copy-start | bytes 1572868
  582.6 8.5 %copy-start.1 = (bf16[256,512]{1,0:T(8,128)(2,1)S(1)}, bf16[256,512]{1,0:T(8,128)(2,1)}, u32[]{:S(2)}) copy-start(bf16[256,512]{1,0:T(8,128)(2,1)} %param.8) | copy-start | bytes 786436
Sparse Core Ops, SparseCore 0:
  358.5 224.0 all-reduce.4
where the time goes:
time: 599 us; the launch traced here: 598 us
  blocking collectives  305 us (51%)
  waiting for transfers between devices  212 us (35%)
  matrix products  43.5 us (7%)
  starting transfers between devices  14.4 us (2%)
  between operations  14.3 us (2%)
  local copies, waits for them, and re-layouts  8.61 us (1%)
    psum x1, waiting for transfers between devices, shards(): lax.psum((grad_blocks, grad_left_local, grad_right_local), 'dp')  168 us
    psum x1, blocking collectives, shards(): reduced = lax.psum(local_low, 'feat').astype(jnp.bfloat16)  162 us
    psum x1, blocking collectives, shards(): back_reduced = lax.psum(local_back, 'feat').astype(jnp.bfloat16)  144 us
    ppermute x10, waiting for transfers between devices, from_partner(): return lax.ppermute(block, axis, route)  43.6 us
    dot_general x16, matrix products, contract(): lax.dot_general(first, second, (((first_dim,), (second_dim,)), ((), ())),...  27.7 us
    ppermute x10, starting transfers between devices, from_partner(): return lax.ppermute(block, axis, route)  14.4 us
  transfers between devices with their start and end apart: 11, of which 4 were waited for; matrix products, arithmetic and copies ran while one was open for 3% of the time, Pallas kernels for 0%

commit v1 on v0

v1 whole, which is shorter than its diff:
```python
import jax
import jax.numpy as jnp
from jax import lax
from jax.sharding import PartitionSpec as P

BF = jnp.bfloat16
F32 = jnp.float32


def flip(block, axis, mask):
    count = lax.axis_size(axis)
    return lax.ppermute(block, axis, [(i, i ^ mask) for i in range(count)])


def normal_cdf(value):
    return 0.5 * (1.0 + lax.erf(value * 0.7071067811865476))


def contract(first, second, first_dim, second_dim):
    return lax.dot_general(
        first, second, (((first_dim,), (second_dim,)), ((), ())), preferred_element_type=F32
    )


def sum_over_feat(part):
    count = lax.axis_size("feat")
    rows, width = part.shape
    pieces = part.astype(BF).reshape(count, rows // count, width)
    pieces = lax.all_to_all(pieces, "feat", 0, 0)
    mine = jnp.sum(pieces.astype(F32), axis=0).astype(BF)
    copies = jnp.broadcast_to(mine[None], (count, rows // count, width))
    return lax.all_to_all(copies, "feat", 0, 0).reshape(rows, width)


def shards(tokens, butterfly, left_factor, right_factor, cotangent):
    bs = tokens.shape[1]
    rows = tokens.shape[0]
    half = rows // 2
    core = lax.axis_index("dp") & 1

    def weight_block(slot):
        return butterfly[:, slot * bs : (slot + 1) * bs]

    first, second = tokens[:half], tokens[half:]
    t0 = flip(tokens, "feat", 1)
    t1a, t3a = flip(first, "feat", 2), flip(first, "feat", 8)
    t1b, t3b = flip(second, "feat", 2), flip(second, "feat", 8)
    t2b, t4b = flip(second, "feat", 4), flip(second, "feat", 16)
    reduced = sum_over_feat(jnp.dot(tokens, left_factor, preferred_element_type=F32))
    t2a, t4a = flip(t1a, "feat", 6), flip(t3a, "feat", 24)

    def both(a, b):
        return jnp.concatenate([a, b], axis=0)

    blocks = [tokens, t0, both(t1a, t1b), both(t2a, t2b), both(t3a, t3b), both(t4a, t4b)]
    pre = jnp.dot(reduced, right_factor, preferred_element_type=F32)
    for slot, block in enumerate(blocks):
        pre = pre + jnp.dot(block, weight_block(slot), preferred_element_type=F32)
    cdf = normal_cdf(pre)
    output = (pre * cdf).astype(BF)
    density = jnp.exp(-0.5 * pre * pre) * 0.3989422804014327
    delta = (cotangent.astype(F32) * (cdf + pre * density)).astype(BF)

    back = contract(delta, weight_block(0), 1, 1)
    sent = []
    for level in (0, 2, 4, 1, 3):
        part = contract(delta, weight_block(level + 1), 1, 1).astype(BF)
        sent.append(flip(part, "feat", 1 << level))

    hc = bs // 2
    keep = lax.dynamic_slice_in_dim(delta, core * hc, hc, 1)
    give = lax.dynamic_slice_in_dim(delta, (1 - core) * hc, hc, 1)

    def over_dp(lefts, give, keep):
        got = flip(jnp.concatenate([contract(l, give, 0, 0) for l in lefts], 0).astype(BF), "dp", 1)
        mine = jnp.concatenate([contract(l, keep, 0, 0) for l in lefts], 0)
        mine = (mine + got.astype(F32)).astype(BF)
        total = mine.astype(F32) + flip(mine, "dp", 2).astype(F32)
        other = flip(total, "dp", 1)
        return jnp.where(core == 0, total, other), jnp.where(core == 0, other, total)

    lo1, hi1 = over_dp(blocks[:3], give, keep)
    lo2, hi2 = over_dp(blocks[3:] + [reduced], give, keep)

    back_reduced = sum_over_feat(contract(delta, right_factor, 1, 1))
    hr = back_reduced.shape[1] // 2
    keep_l = lax.dynamic_slice_in_dim(back_reduced, core * hr, hr, 1)
    give_l = lax.dynamic_slice_in_dim(back_reduced, (1 - core) * hr, hr, 1)
    lo3, hi3 = over_dp([tokens], give_l, keep_l)
    grad_left = jnp.concatenate([lo3, hi3], 1)
    grad_right = jnp.concatenate([lo2[3 * bs :], hi2[3 * bs :]], 1)
    parts = []
    for lo, hi in ((lo1, hi1), (lo2, hi2)):
        for k in range(3):
            parts += [lo[k * bs : (k + 1) * bs], hi[k * bs : (k + 1) * bs]]
    grad_butterfly = jnp.concatenate(parts, 1)

    back = back + contract(back_reduced, left_factor, 1, 1)
    for part in sent:
        back = back + part.astype(F32)
    return (output, back.astype(BF), grad_butterfly, grad_left, grad_right)


def solution(mesh):
    in_specs = (P("dp", "feat"), P("feat", None), P("feat", None), P(None, "feat"), P("dp", "feat"))
    out_specs = (
        P("dp", "feat"),
        P("dp", "feat"),
        P("feat", None),
        P("feat", None),
        P(None, "feat"),
    )
    return jax.shard_map(shards, mesh=mesh, in_specs=in_specs, out_specs=out_specs, check_vma=False)
```

time: 599 us -> 225 us (0.38)
  blocking collectives: 305 us -> 0 us
  waiting for transfers between devices: 212 us -> 58.4 us
  starting transfers between devices: 14.4 us -> 65 us
  local copies, waits for them, and re-layouts: 8.61 us -> 32.7 us
  between operations: 14.3 us -> 1.16 us
  other arithmetic: 0 us -> 12.1 us
  matrix products: 43.5 us -> 54.1 us
    psum x2 -> x0, blocking collectives: 305 us -> none  [the longest x1 162 us: shards(): reduced = lax.psum(local_low, 'feat').astype(jnp.bfloat16)]
    psum x1 -> x0, waiting for transfers between devices: 168 us -> none  [shards(): lax.psum((grad_blocks, grad_left_local, grad_right_local), 'dp')]
    ppermute x10 -> x23, starting transfers between devices: 14.4 us -> 40.6 us  [flip(): return lax.ppermute(block, axis, [(i, i ^ mask) for i in range(count)])]
    all_to_all x0 -> x4, starting transfers between devices: none -> 24.4 us  [the longest x2 15.9 us: sum_over_feat(): pieces = lax.all_to_all(pieces, 'feat', 0, 0)]
    all_to_all x0 -> x4, waiting for transfers between devices: none -> 16 us  [the longest x2 14 us: sum_over_feat(): return lax.all_to_all(copies, 'feat', 0, 0).reshape(rows, width)]
    unnamed x21 -> x68, local copies, waits for them, and re-layouts: 8.61 us -> 23.5 us
    dot_general x16 -> x24, matrix products: 27.7 us -> 36.9 us  [contract(): lax.dot_general(first, second, (((first_dim,), (second_dim,)), ((), ())),...]
    ppermute x10 -> x23, waiting for transfers between devices: 43.6 us -> 42.4 us  [flip(): return lax.ppermute(block, axis, [(i, i ^ mask) for i in range(count)])]
  transfers between devices with their start and end apart: 11 -> 27, of which waited for: 4 -> 8; matrix products, arithmetic and copies ran while one was open for 3% -> 23% of each run, Pallas kernels for 0% -> 0%
where the time goes in v1:
time: 225 us; the launch traced here: 223 us
  starting transfers between devices  65 us (29%)
  waiting for transfers between devices  58.4 us (26%)
  matrix products  54.1 us (24%)
  local copies, waits for them, and re-layouts  32.7 us (15%)
  other arithmetic  12.1 us (5%)
    ppermute x23, waiting for transfers between devices, flip(): return lax.ppermute(block, axis, [(i, i ^ mask) for i in range(count)])  42.4 us
    ppermute x23, starting transfers between devices, flip(): return lax.ppermute(block, axis, [(i, i ^ mask) for i in range(count)])  40.6 us
    dot_general x24, matrix products, contract(): lax.dot_general(first, second, (((first_dim,), (second_dim,)), ((), ())),...  36.9 us
    unnamed x68, local copies, waits for them, and re-layouts  23.5 us
    all_to_all x2, starting transfers between devices, sum_over_feat(): pieces = lax.all_to_all(pieces, 'feat', 0, 0)  15.9 us
    dot_general x6, matrix products, shards(): pre = pre + jnp.dot(block, weight_block(slot), preferred_element_type=F32)  15.6 us
    all_to_all x2, waiting for transfers between devices, sum_over_feat(): return lax.all_to_all(copies, 'feat', 0, 0).reshape(rows, width)  14 us
    all_to_all x2, starting transfers between devices, sum_over_feat(): return lax.all_to_all(copies, 'feat', 0, 0).reshape(rows, width)  8.51 us
  transfers between devices with their start and end apart: 27, of which 8 were waited for; matrix products, arithmetic and copies ran while one was open for 23% of the time, Pallas kernels for 0%

profile of v1, /device:TPU:1, one launch (start us, length us, event | category | flops | bytes accessed | tf_op | source)
XLA Modules:
  0.0 223.5 jit_solution(9465634167813757148)
XLA Ops:
  6.4 8.7 %all-to-all-start = ((bf16[32,32,256]{2,1,0:T(8,128)(2,1)}), bf16[32,32,256]{2,1,0:T(8,128)(2,1)S(1)}, u32[]{:S(2)}, u32[]{:S(2)}) async-start(bf16[32,32,256]{2,1,0:T(8,128)(2,1)} %bitcast), calls=%async_computation | async-start | bytes 1048576 | tf_op jit(solution)/shard_map/all_to_all | solution.py:29
  22.4 3.1 %fusion.30 = f32[1024,512]{1,0:T(8,128)} fusion(bf16[1024,512]{1,0:T(8,128)(2,1)S(1)} %copy-done.2, bf16[512,3072]{1,0:T(8,128)(2,1)} %param.6), kind=kOutput, calls=%fused_computation.75 | convolution fusion | flops 536870912 | bytes 3670016 | tf_op jit(solution)/shard_map/dot_general | solution.py:58
  28.5 3.9 %all-to-all-start.1 = ((bf16[32,32,256]{2,1,0:T(8,128)(2,1)}), bf16[32,32,256]{2,1,0:T(8,128)(2,1)S(1)}, u32[]{:S(2)}, u32[]{:S(2)}) async-start(bf16[32,32,256]{2,1,0:T(8,128)(2,1)} %broadcast_in_dim.4), calls=%async_computation.1 | async-start | bytes 1048576 | tf_op jit(solution)/shard_map/all_to_all | solution.py:32
  34.9 2.6 %collective-permute-start.3 = (bf16[512,512]{1,0:T(8,128)(2,1)}, bf16[512,512]{1,0:T(8,128)(2,1)}, u32[]{:S(2)}, u32[]{:S(2)}) collective-permute-start(bf16[512,512]{1,0:T(8,128)(2,1)} %collective-permute-done.1), channel_id=1, source_target_pairs={{0,6},{1,7},{2,4},{3,5},{4,2},{5,3},{6,0},{7,1},{8,14},{9,15},{10,... | collective-permute-start | bytes 1572872 | tf_op jit(solution)/shard_map/ppermute | solution.py:12
  38.7 3.4 %fusion.17 = f32[1024,512]{1,0:T(8,128)} fusion(bf16[1024,512]{1,0:T(8,128)(2,1)S(1)} %constant_dynamic-update-slice_fusion.4, bf16[512,3072]{1,0:T(8,128)(2,1)} %param.6), kind=kOutput, calls=%fused_computation.62 | convolution fusion | flops 536870912 | bytes 3670016 | tf_op jit(solution)/shard_map/dot_general | solution.py:58
  43.2 18.5 %collective-permute-done.2 = bf16[512,512]{1,0:T(8,128)(2,1)S(1)} collective-permute-done((bf16[512,512]{1,0:T(8,128)(2,1)}, bf16[512,512]{1,0:T(8,128)(2,1)S(1)}, u32[]{:S(2)}, u32[]{:S(2)}) %collective-permute-start.2) | collective-permute-done | bytes 524320 | tf_op jit(solution)/shard_map/ppermute | solution.py:12
  61.7 3.5 %fusion.23 = f32[1024,512]{1,0:T(8,128)} fusion(bf16[1024,512]{1,0:T(8,128)(2,1)S(1)} %constant_dynamic-update-slice_fusion, bf16[512,3072]{1,0:T(8,128)(2,1)} %param.6), kind=kOutput, calls=%fused_computation.68 | convolution fusion | flops 536870912 | bytes 3670016 | tf_op jit(solution)/shard_map/dot_general | solution.py:58
  65.2 3.0 %collective-permute-start.7 = (bf16[512,512]{1,0:T(8,128)(2,1)S(1)}, bf16[512,512]{1,0:T(8,128)(2,1)S(1)}, u32[]{:S(2)}, u32[]{:S(2)}) collective-permute-start(bf16[512,512]{1,0:T(8,128)(2,1)S(1)} %collective-permute-done.5), channel_id=1, source_target_pairs={{0,24},{1,25},{2,26},{3,27},{4,28},{5,29},{6,30},{7,31},{8,16},{9,... | collective-permute-start | bytes 1572872 | tf_op jit(solution)/shard_map/ppermute | solution.py:12
  71.8 6.9 %collective-permute-done.7 = bf16[512,512]{1,0:T(8,128)(2,1)S(1)} collective-permute-done((bf16[512,512]{1,0:T(8,128)(2,1)S(1)}, bf16[512,512]{1,0:T(8,128)(2,1)S(1)}, u32[]{:S(2)}, u32[]{:S(2)}) %collective-permute-start.7) | collective-permute-done | bytes 524320 | tf_op jit(solution)/shard_map/ppermute | solution.py:12
  82.0 2.8 %fusion.5 = (bf16[1024,512]{1,0:T(8,128)(2,1)S(1)}, bf16[1024,512]{1,0:T(8,128)(2,1)}) fusion(bf16[1024,512]{1,0:T(8,128)(2,1)S(1)} %copy-done.15, bf16[1024,512]{1,0:T(8,128)(2,1)S(1)} %constant_dynamic-update-slice_fusion.6, bf16[512,3072]{1,0:T(8,128)(2,1)S(1)} %copy-done.11, f32[1024,512]{1,0:T(8,128)S(1)} %copy-done.4, f32[1024,512]{1,0:T(8,128)S(1)} %fusion.20, ...), kind=kOutput, calls=%fused_computation.6 | convolution fusion | flops 546832384 | bytes 17301504 | tf_op jit(solution)/shard_map/dot_general | solution.py:58
  107.5 7.2 %all-to-all-start.2 = ((bf16[32,32,256]{2,1,0:T(8,128)(2,1)}), bf16[32,32,256]{2,1,0:T(8,128)(2,1)S(1)}, u32[]{:S(2)}, u32[]{:S(2)}) async-start(bf16[32,32,256]{2,1,0:T(8,128)(2,1)} %bitcast.2), calls=%async_computation.2 | async-start | bytes 1048576 | tf_op jit(solution)/shard_map/all_to_all | solution.py:29
  122.3 2.7 %collective-permute-start.10 = (bf16[1024,512]{1,0:T(8,128)(2,1)}, bf16[1024,512]{1,0:T(8,128)(2,1)}, u32[]{:S(2)}, u32[]{:S(2)}) collective-permute-start(bf16[1024,512]{1,0:T(8,128)(2,1)} %convolution_convert_fusion.3), channel_id=1, source_target_pairs={{0,4},{1,5},{2,6},{3,7},{4,0},{5,1},{6,2},{7,3},{8,12},{9,13},{10,... | collective-permute-start | bytes 3145736 | tf_op jit(solution)/shard_map/ppermute | solution.py:12
  125.0 2.7 %collective-permute-start.11 = (bf16[1024,512]{1,0:T(8,128)(2,1)}, bf16[1024,512]{1,0:T(8,128)(2,1)}, u32[]{:S(2)}, u32[]{:S(2)}) collective-permute-start(bf16[1024,512]{1,0:T(8,128)(2,1)} %convolution_convert_fusion.2), channel_id=1, source_target_pairs={{0,16},{1,17},{2,18},{3,19},{4,20},{5,21},{6,22},{7,23},{8,24},{9,... | collective-permute-start | bytes 3145736 | tf_op jit(solution)/shard_map/ppermute | solution.py:12
  128.8 3.1 %fusion.28 = f32[1024,512]{1,0:T(8,128)} fusion(bf16[1024,512]{1,0:T(8,128)(2,1)S(1)} %get-tuple-element.14, bf16[512,3072]{1,0:T(8,128)(2,1)} %param.6), kind=kOutput, calls=%fused_computation.73 | convolution fusion | flops 536870912 | bytes 3670016 | tf_op jit(solution)/shard_map/dot_general | solution.py:20
  132.8 4.6 %all-to-all-start.3 = ((bf16[32,32,256]{2,1,0:T(8,128)(2,1)}), bf16[32,32,256]{2,1,0:T(8,128)(2,1)}, u32[]{:S(2)}, u32[]{:S(2)}) async-start(bf16[32,32,256]{2,1,0:T(8,128)(2,1)} %broadcast_in_dim.5), calls=%async_computation.3 | async-start | bytes 1048576 | tf_op jit(solution)/shard_map/all_to_all | solution.py:32
  140.9 2.5 %collective-permute-start.15 = (bf16[1536,256]{0,1:T(8,128)(2,1)S(1)}, bf16[1536,256]{0,1:T(8,128)(2,1)}, u32[]{:S(2)}, u32[]{:S(2)}) collective-permute-start(bf16[1536,256]{0,1:T(8,128)(2,1)S(1)} %fusion.7), channel_id=1, source_target_pairs={{0,64},{32,96},{64,0},{96,32},{1,65},{33,97},{65,1},{97,33},{2,66}... | collective-permute-start | bytes 2359304 | tf_op jit(solution)/shard_map/ppermute | solution.py:12
  143.4 14.0 %all-to-all-done.3 = bf16[32,32,256]{2,1,0:T(8,128)(2,1)} async-done(((bf16[32,32,256]{2,1,0:T(8,128)(2,1)}), bf16[32,32,256]{2,1,0:T(8,128)(2,1)}, u32[]{:S(2)}, u32[]{:S(2)}) %all-to-all-start.3) | async-done | bytes 524320 | tf_op jit(solution)/shard_map/all_to_all | solution.py:32
  165.2 5.1 %collective-permute-done.15 = bf16[1536,256]{0,1:T(8,128)(2,1)} collective-permute-done((bf16[1536,256]{0,1:T(8,128)(2,1)S(1)}, bf16[1536,256]{0,1:T(8,128)(2,1)}, u32[]{:S(2)}, u32[]{:S(2)}) %collective-permute-start.15) | collective-permute-done | bytes 786464 | tf_op jit(solution)/shard_map/ppermute | solution.py:12
  170.8 2.5 %convert_add_fusion.1 = f32[1536,256]{0,1:T(8,128)} fusion(bf16[1536,256]{0,1:T(8,128)(2,1)} %collective-permute-done.15, bf16[1536,256]{0,1:T(8,128)(2,1)S(1)} %fusion.7), kind=kLoop, calls=%fused_computation.16 | loop fusion | flops 1179648 | bytes 3145728 | tf_op jit(solution)/shard_map/add | solution.py:78
  178.3 8.2 %collective-permute-done.12 = bf16[1024,512]{1,0:T(8,128)(2,1)S(1)} collective-permute-done((bf16[1024,512]{1,0:T(8,128)(2,1)S(1)}, bf16[1024,512]{1,0:T(8,128)(2,1)S(1)}, u32[]{:S(2)}, u32[]{:S(2)}) %collective-permute-start.12) | collective-permute-done | bytes 1048608 | tf_op jit(solution)/shard_map/ppermute | solution.py:12
  186.9 4.0 %add_convert_fusion = bf16[1024,512]{1,0:T(8,128)(2,1)} fusion(bf16[1024,512]{1,0:T(8,128)(2,1)S(1)} %collective-permute-done.13, bf16[1024,512]{1,0:T(8,128)(2,1)S(1)} %collective-permute-done.12, bf16[1024,512]{1,0:T(8,128)(2,1)} %collective-permute-done.11, bf16[1024,512]{1,0:T(8,128)(2,1)} %collective-permute-done.10, ...), kind=kOutput, calls=%fused_computation.7 | convolution fusion | flops 274726912 | bytes 9175040 | tf_op jit(solution)/shard_map/dot_general | solution.py:20
  192.0 3.3 %collective-permute-done.18 = bf16[1792,256]{0,1:T(8,128)(2,1)S(1)} collective-permute-done((bf16[1792,256]{0,1:T(8,128)(2,1)S(1)}, bf16[1792,256]{0,1:T(8,128)(2,1)S(1)}, u32[]{:S(2)}, u32[]{:S(2)}) %collective-permute-start.18) | collective-permute-done | bytes 917536 | tf_op jit(solution)/shard_map/ppermute | solution.py:12
  195.5 2.5 %collective-permute-start.19 = (f32[1792,256]{0,1:T(8,128)S(1)}, f32[1792,256]{0,1:T(8,128)S(1)}, u32[]{:S(2)}, u32[]{:S(2)}) collective-permute-start(f32[1792,256]{0,1:T(8,128)S(1)} %convert_add_fusion), channel_id=1, source_target_pairs={{0,32},{32,0},{64,96},{96,64},{1,33},{33,1},{65,97},{97,65},{2,34}... | collective-permute-start | bytes 5505032 | tf_op jit(solution)/shard_map/ppermute | solution.py:12
  216.9 6.6 %copy.20 = f32[512,3072]{1,0:T(8,128)} copy(f32[512,3072]{0,1:T(8,128)} %slice_dynamic-update-slice_fusion) | data formatting | bytes 12582912
  (154 shorter events, 96.9 us)
Async XLA Ops:
  3.0 29.3 %collective-permute-start.5 = (bf16[512,512]{1,0:T(8,128)(2,1)}, bf16[512,512]{1,0:T(8,128)(2,1)S(1)}, u32[]{:S(2)}, u32[]{:S(2)}) collective-permute-start(bf16[512,512]{1,0:T(8,128)(2,1)} %get-tuple-element.17), channel_id=1, source_target_pairs={{0,8},{1,9},{2,10},{3,11},{4,12},{5,13},{6,14},{7,15},{8,0},{9,1},... | collective-permute-start | bytes 1572872 | tf_op jit(solution)/shard_map/ppermute | solution.py:12
  6.4 21.1 %all-to-all-start = ((bf16[32,32,256]{2,1,0:T(8,128)(2,1)}), bf16[32,32,256]{2,1,0:T(8,128)(2,1)S(1)}, u32[]{:S(2)}, u32[]{:S(2)}) async-start(bf16[32,32,256]{2,1,0:T(8,128)(2,1)} %bitcast), calls=%async_computation | async-start | bytes 1048576 | tf_op jit(solution)/shard_map/all_to_all | solution.py:29
  15.1 18.6 %collective-permute-start.1 = (bf16[512,512]{1,0:T(8,128)(2,1)}, bf16[512,512]{1,0:T(8,128)(2,1)}, u32[]{:S(2)}, u32[]{:S(2)}) collective-permute-start(bf16[512,512]{1,0:T(8,128)(2,1)} %get-tuple-element.17), channel_id=1, source_target_pairs={{0,2},{1,3},{2,0},{3,1},{4,6},{5,7},{6,4},{7,5},{8,10},{9,11},{10,... | collective-permute-start | bytes 1572872 | tf_op jit(solution)/shard_map/ppermute | solution.py:12
  16.4 18.5 %collective-permute-start.6 = (bf16[512,512]{1,0:T(8,128)(2,1)}, bf16[512,512]{1,0:T(8,128)(2,1)}, u32[]{:S(2)}, u32[]{:S(2)}) collective-permute-start(bf16[512,512]{1,0:T(8,128)(2,1)} %get-tuple-element.16), channel_id=1, source_target_pairs={{0,8},{1,9},{2,10},{3,11},{4,12},{5,13},{6,14},{7,15},{8,0},{9,1},... | collective-permute-start | bytes 1572872 | tf_op jit(solution)/shard_map/ppermute | solution.py:12
  17.6 63.3 %collective-permute-start.8 = (bf16[512,512]{1,0:T(8,128)(2,1)}, bf16[512,512]{1,0:T(8,128)(2,1)}, u32[]{:S(2)}, u32[]{:S(2)}) collective-permute-start(bf16[512,512]{1,0:T(8,128)(2,1)} %get-tuple-element.16), channel_id=1, source_target_pairs={{0,16},{1,17},{2,18},{3,19},{4,20},{5,21},{6,22},{7,23},{8,24},{9,... | collective-permute-start | bytes 1572872 | tf_op jit(solution)/shard_map/ppermute | solution.py:12
  20.0 49.9 %collective-permute-start.4 = (bf16[512,512]{1,0:T(8,128)(2,1)}, bf16[512,512]{1,0:T(8,128)(2,1)}, u32[]{:S(2)}, u32[]{:S(2)}) collective-permute-start(bf16[512,512]{1,0:T(8,128)(2,1)} %get-tuple-element.16), channel_id=1, source_target_pairs={{0,4},{1,5},{2,6},{3,7},{4,0},{5,1},{6,2},{7,3},{8,12},{9,13},{10,... | collective-permute-start | bytes 1572872 | tf_op jit(solution)/shard_map/ppermute | solution.py:12
  28.5 39.8 %all-to-all-start.1 = ((bf16[32,32,256]{2,1,0:T(8,128)(2,1)}), bf16[32,32,256]{2,1,0:T(8,128)(2,1)S(1)}, u32[]{:S(2)}, u32[]{:S(2)}) async-start(bf16[32,32,256]{2,1,0:T(8,128)(2,1)} %broadcast_in_dim.4), calls=%async_computation.1 | async-start | bytes 1048576 | tf_op jit(solution)/shard_map/all_to_all | solution.py:32
  32.4 29.3 %collective-permute-start.2 = (bf16[512,512]{1,0:T(8,128)(2,1)}, bf16[512,512]{1,0:T(8,128)(2,1)S(1)}, u32[]{:S(2)}, u32[]{:S(2)}) collective-permute-start(bf16[512,512]{1,0:T(8,128)(2,1)} %get-tuple-element.16), channel_id=1, source_target_pairs={{0,2},{1,3},{2,0},{3,1},{4,6},{5,7},{6,4},{7,5},{8,10},{9,11},{10,... | collective-permute-start | bytes 1572872 | tf_op jit(solution)/shard_map/ppermute | solution.py:12
  33.7 45.1 %collective-permute-start = (bf16[1024,512]{1,0:T(8,128)(2,1)S(1)}, bf16[1024,512]{1,0:T(8,128)(2,1)}, u32[]{:S(2)}, u32[]{:S(2)}) collective-permute-start(bf16[1024,512]{1,0:T(8,128)(2,1)S(1)} %copy-done.2), channel_id=1, source_target_pairs={{0,1},{1,0},{2,3},{3,2},{4,5},{5,4},{6,7},{7,6},{8,9},{9,8},{10,11... | collective-permute-start | bytes 3145736 | tf_op jit(solution)/shard_map/ppermute | solution.py:12
  34.9 33.7 %collective-permute-start.3 = (bf16[512,512]{1,0:T(8,128)(2,1)}, bf16[512,512]{1,0:T(8,128)(2,1)}, u32[]{:S(2)}, u32[]{:S(2)}) collective-permute-start(bf16[512,512]{1,0:T(8,128)(2,1)} %collective-permute-done.1), channel_id=1, source_target_pairs={{0,6},{1,7},{2,4},{3,5},{4,2},{5,3},{6,0},{7,1},{8,14},{9,15},{10,... | collective-permute-start | bytes 1572872 | tf_op jit(solution)/shard_map/ppermute | solution.py:12
  65.2 13.5 %collective-permute-start.7 = (bf16[512,512]{1,0:T(8,128)(2,1)S(1)}, bf16[512,512]{1,0:T(8,128)(2,1)S(1)}, u32[]{:S(2)}, u32[]{:S(2)}) collective-permute-start(bf16[512,512]{1,0:T(8,128)(2,1)S(1)} %collective-permute-done.5), channel_id=1, source_target_pairs={{0,24},{1,25},{2,26},{3,27},{4,28},{5,29},{6,30},{7,31},{8,16},{9,... | collective-permute-start | bytes 1572872 | tf_op jit(solution)/shard_map/ppermute | solution.py:12
  107.5 24.3 %all-to-all-start.2 = ((bf16[32,32,256]{2,1,0:T(8,128)(2,1)}), bf16[32,32,256]{2,1,0:T(8,128)(2,1)S(1)}, u32[]{:S(2)}, u32[]{:S(2)}) async-start(bf16[32,32,256]{2,1,0:T(8,128)(2,1)} %bitcast.2), calls=%async_computation.2 | async-start | bytes 1048576 | tf_op jit(solution)/shard_map/all_to_all | solution.py:29
  117.6 21.6 %collective-permute-start.14 = (bf16[1536,256]{0,1:T(8,128)(2,1)}, bf16[1536,256]{0,1:T(8,128)(2,1)}, u32[]{:S(2)}, u32[]{:S(2)}) collective-permute-start(bf16[1536,256]{0,1:T(8,128)(2,1)} %pad_maximum_fusion.1), channel_id=1, source_target_pairs={{0,32},{32,0},{64,96},{96,64},{1,33},{33,1},{65,97},{97,65},{2,34}... | collective-permute-start | bytes 2359304 | tf_op jit(solution)/shard_map/ppermute | solution.py:12
  120.8 37.9 %collective-permute-start.17 = (bf16[1792,256]{0,1:T(8,128)(2,1)}, bf16[1792,256]{0,1:T(8,128)(2,1)}, u32[]{:S(2)}, u32[]{:S(2)}) collective-permute-start(bf16[1792,256]{0,1:T(8,128)(2,1)} %pad_maximum_fusion), channel_id=1, source_target_pairs={{0,32},{32,0},{64,96},{96,64},{1,33},{33,1},{65,97},{97,65},{2,34}... | collective-permute-start | bytes 2752520 | tf_op jit(solution)/shard_map/ppermute | solution.py:12
  120.8 41.0 %collective-permute-start.9 = (bf16[1024,512]{1,0:T(8,128)(2,1)}, bf16[1024,512]{1,0:T(8,128)(2,1)}, u32[]{:S(2)}, u32[]{:S(2)}) collective-permute-start(bf16[1024,512]{1,0:T(8,128)(2,1)} %convolution_convert_fusion.4), channel_id=1, source_target_pairs={{0,1},{1,0},{2,3},{3,2},{4,5},{5,4},{6,7},{7,6},{8,9},{9,8},{10,11... | collective-permute-start | bytes 3145736 | tf_op jit(solution)/shard_map/ppermute | solution.py:12
  122.3 51.0 %collective-permute-start.10 = (bf16[1024,512]{1,0:T(8,128)(2,1)}, bf16[1024,512]{1,0:T(8,128)(2,1)}, u32[]{:S(2)}, u32[]{:S(2)}) collective-permute-start(bf16[1024,512]{1,0:T(8,128)(2,1)} %convolution_convert_fusion.3), channel_id=1, source_target_pairs={{0,4},{1,5},{2,6},{3,7},{4,0},{5,1},{6,2},{7,3},{8,12},{9,13},{10,... | collective-permute-start | bytes 3145736 | tf_op jit(solution)/shard_map/ppermute | solution.py:12
  125.0 53.2 %collective-permute-start.11 = (bf16[1024,512]{1,0:T(8,128)(2,1)}, bf16[1024,512]{1,0:T(8,128)(2,1)}, u32[]{:S(2)}, u32[]{:S(2)}) collective-permute-start(bf16[1024,512]{1,0:T(8,128)(2,1)} %convolution_convert_fusion.2), channel_id=1, source_target_pairs={{0,16},{1,17},{2,18},{3,19},{4,20},{5,21},{6,22},{7,23},{8,24},{9,... | collective-permute-start | bytes 3145736 | tf_op jit(solution)/shard_map/ppermute | solution.py:12
  132.8 24.5 %all-to-all-start.3 = ((bf16[32,32,256]{2,1,0:T(8,128)(2,1)}), bf16[32,32,256]{2,1,0:T(8,128)(2,1)}, u32[]{:S(2)}, u32[]{:S(2)}) async-start(bf16[32,32,256]{2,1,0:T(8,128)(2,1)} %broadcast_in_dim.5), calls=%async_computation.3 | async-start | bytes 1048576 | tf_op jit(solution)/shard_map/all_to_all | solution.py:32
  140.9 29.4 %collective-permute-start.15 = (bf16[1536,256]{0,1:T(8,128)(2,1)S(1)}, bf16[1536,256]{0,1:T(8,128)(2,1)}, u32[]{:S(2)}, u32[]{:S(2)}) collective-permute-start(bf16[1536,256]{0,1:T(8,128)(2,1)S(1)} %fusion.7), channel_id=1, source_target_pairs={{0,64},{32,96},{64,0},{96,32},{1,65},{33,97},{65,1},{97,33},{2,66}... | collective-permute-start | bytes 2359304 | tf_op jit(solution)/shard_map/ppermute | solution.py:12
  161.8 24.7 %collective-permute-start.12 = (bf16[1024,512]{1,0:T(8,128)(2,1)S(1)}, bf16[1024,512]{1,0:T(8,128)(2,1)S(1)}, u32[]{:S(2)}, u32[]{:S(2)}) collective-permute-start(bf16[1024,512]{1,0:T(8,128)(2,1)S(1)} %copy-done.24), channel_id=1, source_target_pairs={{0,2},{1,3},{2,0},{3,1},{4,6},{5,7},{6,4},{7,5},{8,10},{9,11},{10,... | collective-permute-start | bytes 3145736 | tf_op jit(solution)/shard_map/ppermute | solution.py:12
  162.6 24.3 %collective-permute-start.13 = (bf16[1024,512]{1,0:T(8,128)(2,1)S(1)}, bf16[1024,512]{1,0:T(8,128)(2,1)S(1)}, u32[]{:S(2)}, u32[]{:S(2)}) collective-permute-start(bf16[1024,512]{1,0:T(8,128)(2,1)S(1)} %copy-done.23), channel_id=1, source_target_pairs={{0,8},{1,9},{2,10},{3,11},{4,12},{5,13},{6,14},{7,15},{8,0},{9,1},... | collective-permute-start | bytes 3145736 | tf_op jit(solution)/shard_map/ppermute | solution.py:12
  173.4 22.0 %collective-permute-start.18 = (bf16[1792,256]{0,1:T(8,128)(2,1)S(1)}, bf16[1792,256]{0,1:T(8,128)(2,1)S(1)}, u32[]{:S(2)}, u32[]{:S(2)}) collective-permute-start(bf16[1792,256]{0,1:T(8,128)(2,1)S(1)} %fusion.6), channel_id=1, source_target_pairs={{0,64},{32,96},{64,0},{96,32},{1,65},{33,97},{65,1},{97,33},{2,66}... | collective-permute-start | bytes 2752520 | tf_op jit(solution)/shard_map/ppermute | solution.py:12
  175.8 22.2 %collective-permute-start.16 = (f32[1536,256]{0,1:T(8,128)}, f32[1536,256]{0,1:T(8,128)}, u32[]{:S(2)}, u32[]{:S(2)}) collective-permute-start(f32[1536,256]{0,1:T(8,128)} %convert_add_fusion.1), channel_id=1, source_target_pairs={{0,32},{32,0},{64,96},{96,64},{1,33},{33,1},{65,97},{97,65},{2,34}... | collective-permute-start | bytes 4718600 | tf_op jit(solution)/shard_map/ppermute | solution.py:12
  178.2 12.7 %collective-permute-start.22 = (f32[512,128]{0,1:T(8,128)S(1)}, f32[512,128]{0,1:T(8,128)S(1)}, u32[]{:S(2)}, u32[]{:S(2)}) collective-permute-start(f32[512,128]{0,1:T(8,128)S(1)} %convert_add_fusion.2), channel_id=1, source_target_pairs={{0,32},{32,0},{64,96},{96,64},{1,33},{33,1},{65,97},{97,65},{2,34}... | collective-permute-start | bytes 786440 | tf_op jit(solution)/shard_map/ppermute | solution.py:12
  (28 other events, 244.7 us)

commit v2 on v0

v2 whole, which is shorter than its diff:
```python
import functools

import jax
import jax.numpy as jnp
from jax import lax
from jax.experimental import pallas as pl
from jax.experimental.pallas import tpu as pltpu
from jax.sharding import PartitionSpec as P

BF = jnp.bfloat16
F32 = jnp.float32
TILE = 256


def flip(block, axis, mask):
    count = lax.axis_size(axis)
    return lax.ppermute(block, axis, [(i, i ^ mask) for i in range(count)])


def normal_cdf(value):
    return 0.5 * (1.0 + lax.erf(value * 0.7071067811865476))


def contract(first, second, first_dim, second_dim):
    return lax.dot_general(
        first, second, (((first_dim,), (second_dim,)), ((), ())), preferred_element_type=F32
    )


def struct(*shape_and_type):
    *shape, kind = shape_and_type
    return jax.ShapeDtypeStruct(tuple(shape), kind)


def call(kernel, outs, *args, name, vmem=40, **more):
    return pl.pallas_call(
        kernel,
        out_shape=outs,
        name=name,
        compiler_params=pltpu.CompilerParams(vmem_limit_bytes=vmem << 20),
        cost_estimate=pl.CostEstimate(flops=1000, bytes_accessed=1000, transcendentals=0),
        **more,
    )(*args)


def low_kernel(x, w, o):
    o[...] = jnp.dot(x[...], w[...], preferred_element_type=F32).astype(BF)


def sum_kernel(pieces, copies):
    count = pieces.shape[0]
    total = pieces[0].astype(F32)
    for k in range(1, count):
        total = total + pieces[k].astype(F32)
    mine = total.astype(BF)
    for k in range(count):
        copies[k] = mine


def forward_kernel(slots, reduced, right, cotangent, weight, *refs):
    blocks, (output, delta) = refs[:-2], refs[-2:]
    rows, bs = output.shape
    for row in range(0, rows, TILE):
        here = slice(row, row + TILE)
        pre = jnp.dot(reduced[here, :], right[...], preferred_element_type=F32)
        for slot, parts in enumerate(slots):
            size = rows // len(parts)
            ref = blocks[parts[row // size]]
            inside = slice(row % size, row % size + TILE)
            pre = pre + jnp.dot(
                ref[inside, :], weight[:, slot * bs : (slot + 1) * bs], preferred_element_type=F32
            )
        cdf = normal_cdf(pre)
        output[here, :] = (pre * cdf).astype(BF)
        density = jnp.exp(-0.5 * pre * pre) * 0.3989422804014327
        delta[here, :] = (cotangent[here, :].astype(F32) * (cdf + pre * density)).astype(BF)


def half_dots(slots, blocks, cols, hc):
    out = []
    for parts in slots:
        total = None
        row = 0
        for k in parts:
            term = contract(blocks[k][...], cols[row : row + blocks[k].shape[0], :], 0, 0)
            total = term if total is None else total + term
            row += blocks[k].shape[0]
        out.append(total)
    return out


def give_kernel(slots, core, delta, *refs):
    blocks, out = refs[:-1], refs[-1]
    hc = delta.shape[1] // 2

    def run(cols):
        row = 0
        for total in half_dots(slots, blocks, cols, hc):
            out[row : row + total.shape[0], :] = total.astype(out.dtype)
            row += total.shape[0]

    @pl.when(core[0] == 0)
    def _():
        run(delta[:, hc:])

    @pl.when(core[0] == 1)
    def _():
        run(delta[:, :hc])


def keep_kernel(slots, core, delta, got, *refs):
    blocks, out = refs[:-1], refs[-1]
    hc = delta.shape[1] // 2

    def run(cols):
        row = 0
        for total in half_dots(slots, blocks, cols, hc):
            here = slice(row, row + total.shape[0])
            out[here, :] = (total + got[here, :].astype(F32)).astype(out.dtype)
            row += total.shape[0]

    @pl.when(core[0] == 0)
    def _():
        run(delta[:, :hc])

    @pl.when(core[0] == 1)
    def _():
        run(delta[:, hc:])


def back_kernel(slots, delta, weight, *outs):
    bs = delta.shape[1]
    for slot, out in zip(slots, outs):
        out[...] = contract(delta[...], weight[:, slot * bs : (slot + 1) * bs], 1, 1).astype(
            out.dtype
        )


def local_back_kernel(delta, right, out):
    out[...] = contract(delta[...], right[...], 1, 1).astype(BF)


def finish_kernel(delta, weight, back_reduced, left, *refs):
    parts, out = refs[:-1], refs[-1]
    rows, bs = out.shape
    for row in range(0, rows, TILE):
        here = slice(row, row + TILE)
        total = contract(delta[here, :], weight[:, :bs], 1, 1)
        total = total + contract(back_reduced[here, :], left[...], 1, 1)
        for part in parts:
            total = total + part[here, :].astype(F32)
        out[here, :] = total.astype(BF)


def assemble_kernel(count, with_old, core, *refs):
    mine, recv, mine_o, recv_o = refs[:4]
    outs = refs[4 + with_old :]

    def run(a, b, c, d):
        hc = a.shape[1]
        out = outs[0]
        out[:, :hc] = a[...].astype(F32) + b[...].astype(F32)
        out[:, hc:] = c[...].astype(F32) + d[...].astype(F32)

    @pl.when(core[0] == 0)
    def _():
        run(mine, recv, mine_o, recv_o)

    @pl.when(core[0] == 1)
    def _():
        run(mine_o, recv_o, mine, recv)


def assemble(core, four, out, steps, in_start, out_start, old, name):
    hc = four[0].shape[1]
    bs = out.shape[0]
    half = pl.BlockSpec((bs, hc), lambda k: (k + in_start, 0))
    more = {}
    specs = [pl.BlockSpec(memory_space=pltpu.SMEM)] + [half] * 4
    args = [core, *four]
    if old is not None:
        specs.append(pl.BlockSpec(memory_space=pl.ANY))
        args.append(old)
        more["input_output_aliases"] = {5: 0}
    return call(
        functools.partial(assemble_kernel, steps, old is not None),
        out,
        *args,
        name=name,
        grid=(steps,),
        in_specs=specs,
        out_specs=pl.BlockSpec((bs, 2 * hc), lambda k: (0, k + out_start)),
        **more,
    )


def sum_over_feat(part, name):
    count = lax.axis_size("feat")
    rows, width = part.shape
    shape = (count, rows // count, width)
    pieces = lax.all_to_all(part.reshape(shape), "feat", 0, 0)
    copies = call(sum_kernel, struct(*shape, BF), pieces, name=name)
    return lax.all_to_all(copies, "feat", 0, 0).reshape(rows, width)


def shards(tokens, butterfly, left_factor, right_factor, cotangent):
    rows, bs = tokens.shape
    rank = left_factor.shape[1]
    half = rows // 2
    hc = bs // 2
    core = (lax.axis_index("dp") & 1).astype(jnp.int32).reshape(1)
    smem = pl.BlockSpec(memory_space=pltpu.SMEM)
    whole = pl.BlockSpec()

    first, second = tokens[:half], tokens[half:]
    t0 = flip(tokens, "feat", 1)
    t1a, t3a = flip(first, "feat", 2), flip(first, "feat", 8)
    t1b, t3b = flip(second, "feat", 2), flip(second, "feat", 8)
    t2b, t4b = flip(second, "feat", 4), flip(second, "feat", 16)
    low = call(low_kernel, struct(rows, rank, BF), tokens, left_factor, name="low")
    reduced = sum_over_feat(low, "low_sum")
    t2a, t4a = flip(t1a, "feat", 6), flip(t3a, "feat", 24)

    blocks = (tokens, t0, t1a, t1b, t2a, t2b, t3a, t3b, t4a, t4b)
    slots = ((0,), (1,), (2, 3), (4, 5), (6, 7), (8, 9))
    output, delta = call(
        functools.partial(forward_kernel, slots),
        (struct(rows, bs, BF), struct(rows, bs, BF)),
        reduced,
        right_factor,
        cotangent,
        butterfly,
        *blocks,
        name="forward",
    )

    (c0,) = call(functools.partial(back_kernel, (1,)), (struct(rows, bs, BF),), delta, butterfly, name="back_x")
    r0 = flip(c0, "feat", 1)
    local_back = call(local_back_kernel, struct(rows, rank, BF), delta, right_factor, name="local_back")

    def specs(n):
        return [smem] + [whole] * n

    chunks = (
        ((0,), (1,), (2, 3)),
        ((4, 5), (6, 7), (8, 9), (10,)),
    )
    every = blocks + (reduced,)

    def renumber(chunk):
        used = [k for parts in chunk for k in parts]
        return [every[k] for k in used], tuple(tuple(used.index(k) for k in parts) for parts in chunk)

    gots = []
    for index, chunk in enumerate(chunks):
        used, local = renumber(chunk)
        height = sum(every[parts[0]].shape[1] for parts in chunk)
        give = call(
            functools.partial(give_kernel, local),
            struct(height, hc, BF),
            core,
            delta,
            *used,
            name=f"give{index}",
            in_specs=specs(1 + len(used)),
        )
        gots.append(flip(give, "dp", 1))
    c2, c4, c1, c3 = call(
        functools.partial(back_kernel, (3, 5, 2, 4)),
        (struct(rows, bs, BF),) * 4,
        delta,
        butterfly,
        name="back_yz",
    )
    r2, r4 = flip(c2, "feat", 4), flip(c4, "feat", 16)
    r1, r3 = flip(c1, "feat", 2), flip(c3, "feat", 8)
    fours = []
    for index, chunk in enumerate(chunks):
        used, local = renumber(chunk)
        mine = call(
            functools.partial(keep_kernel, local),
            struct(*gots[index].shape, BF),
            core,
            delta,
            gots[index],
            *used,
            name=f"keep{index}",
            in_specs=specs(2 + len(used)),
        )
        recv = flip(mine, "dp", 2)
        fours.append((mine, recv, flip(mine, "dp", 1), flip(recv, "dp", 1)))

    back_reduced = sum_over_feat(local_back, "back_sum")
    give = call(
        functools.partial(give_kernel, ((0,),)),
        struct(bs, rank // 2, BF),
        core,
        back_reduced,
        tokens,
        name="give_left",
        in_specs=specs(2),
    )
    got = flip(give, "dp", 1)
    mine = call(
        functools.partial(keep_kernel, ((0,),)),
        struct(bs, rank // 2, BF),
        core,
        back_reduced,
        got,
        tokens,
        name="keep_left",
        in_specs=specs(3),
    )
    recv = flip(mine, "dp", 2)
    left_four = (mine, recv, flip(mine, "dp", 1), flip(recv, "dp", 1))

    grads = struct(*butterfly.shape, F32)
    grads_a = assemble(core, fours[0], grads, 3, 0, 0, None, "put0")
    grad_butterfly = assemble(core, fours[1], grads, 3, 0, 3, grads_a, "put1")
    grad_right = assemble(
        core, fours[1], struct(rank, bs, F32), 1, 3 * bs // rank, 0, None, "put_right"
    )
    grad_left = assemble(core, left_four, struct(bs, rank, F32), 1, 0, 0, None, "put_left")

    grad_tokens = call(
        finish_kernel,
        struct(rows, bs, BF),
        delta,
        butterfly,
        back_reduced,
        left_factor,
        r0,
        r1,
        r2,
        r3,
        r4,
        name="finish",
    )
    return (output, grad_tokens, grad_butterfly, grad_left, grad_right)


def solution(mesh):
    in_specs = (P("dp", "feat"), P("feat", None), P("feat", None), P(None, "feat"), P("dp", "feat"))
    out_specs = (
        P("dp", "feat"),
        P("dp", "feat"),
        P("feat", None),
        P("feat", None),
        P(None, "feat"),
    )
    return jax.shard_map(shards, mesh=mesh, in_specs=in_specs, out_specs=out_specs, check_vma=False)
```

time: 599 us -> 200 us (0.33)
  blocking collectives: 305 us -> 15.5 us
  waiting for transfers between devices: 212 us -> 72.8 us
  Pallas kernels: 0 us -> 44.2 us
  matrix products: 43.5 us -> 0 us
  starting transfers between devices: 14.4 us -> 49 us
  between operations: 14.3 us -> 0.88 us
  local copies, waits for them, and re-layouts: 8.61 us -> 16.4 us
    psum x2 -> x0, blocking collectives: 305 us -> none  [the longest x1 162 us: shards(): reduced = lax.psum(local_low, 'feat').astype(jnp.bfloat16)]
    psum x1 -> x0, waiting for transfers between devices: 168 us -> none  [shards(): lax.psum((grad_blocks, grad_left_local, grad_right_local), 'dp')]
    pallas_call x0 -> x18, Pallas kernels: none -> 44.2 us  [call(): pl.pallas_call(kernel, out_shape=outs, name=name, compiler_params=pltpu.C...]
    dot_general x24 -> x0, matrix products: 43.5 us -> none  [the longest x16 27.7 us: contract(): lax.dot_general(first, second, (((first_dim,), (second_dim,)), ((), ())),...]
    all_to_all x0 -> x3, waiting for transfers between devices: none -> 38.1 us  [the longest x2 24.7 us: sum_over_feat(): pieces = lax.all_to_all(part.reshape(shape), 'feat', 0, 0)]
    ppermute x10 -> x26, starting transfers between devices: 14.4 us -> 32.4 us  [flip(): return lax.ppermute(block, axis, [(i, i ^ mask) for i in range(count)])]
    all_to_all x0 -> x3, starting transfers between devices: none -> 16.6 us  [the longest x2 11.1 us: sum_over_feat(): pieces = lax.all_to_all(part.reshape(shape), 'feat', 0, 0)]
    all_to_all x0 -> x1, blocking collectives: none -> 15.5 us  [sum_over_feat(): return lax.all_to_all(copies, 'feat', 0, 0).reshape(rows, width)]
  transfers between devices with their start and end apart: 11 -> 29, of which waited for: 4 -> 8; matrix products, arithmetic and copies ran while one was open for 3% -> 0% of each run, Pallas kernels for 0% -> 14%
where the time goes in v2:
time: 200 us; the launch traced here: 199 us
  waiting for transfers between devices  72.8 us (36%)
  starting transfers between devices  49 us (24%)
  Pallas kernels  44.2 us (22%)
  local copies, waits for them, and re-layouts  16.4 us (8%)
  blocking collectives  15.5 us (8%)
    pallas_call x18, Pallas kernels, call(): pl.pallas_call(kernel, out_shape=outs, name=name, compiler_params=pltpu.C...  44.2 us
    ppermute x26, waiting for transfers between devices, flip(): return lax.ppermute(block, axis, [(i, i ^ mask) for i in range(count)])  34.8 us
    ppermute x26, starting transfers between devices, flip(): return lax.ppermute(block, axis, [(i, i ^ mask) for i in range(count)])  32.4 us
    all_to_all x2, waiting for transfers between devices, sum_over_feat(): pieces = lax.all_to_all(part.reshape(shape), 'feat', 0, 0)  24.7 us
    all_to_all x1, blocking collectives, sum_over_feat(): return lax.all_to_all(copies, 'feat', 0, 0).reshape(rows, width)  15.5 us
    unnamed x46, local copies, waits for them, and re-layouts  14.1 us
    all_to_all x1, waiting for transfers between devices, sum_over_feat(): return lax.all_to_all(copies, 'feat', 0, 0).reshape(rows, width)  13.4 us
    all_to_all x2, starting transfers between devices, sum_over_feat(): pieces = lax.all_to_all(part.reshape(shape), 'feat', 0, 0)  11.1 us
  transfers between devices with their start and end apart: 29, of which 8 were waited for; matrix products, arithmetic and copies ran while one was open for 0% of the time, Pallas kernels for 14%

profile of v2, /device:TPU:1, one launch (start us, length us, event | category | flops | bytes accessed | tf_op | source)
XLA Modules:
  0.0 198.9 jit_solution(17761674528349169233)
XLA Ops:
  3.0 2.5 %collective-permute-start.1 = (bf16[512,512]{1,0:T(8,128)(2,1)}, bf16[512,512]{1,0:T(8,128)(2,1)S(1)}, u32[]{:S(2)}, u32[]{:S(2)}) collective-permute-start(bf16[512,512]{1,0:T(8,128)(2,1)} %get-tuple-element.18), channel_id=1, source_target_pairs={{0,2},{1,3},{2,0},{3,1},{4,6},{5,7},{6,4},{7,5},{8,10},{9,11},{10,... | collective-permute-start | bytes 1572872 | tf_op jit(solution)/shard_map/ppermute | solution.py:17
  5.5 3.4 %collective-permute-start.4 = (bf16[512,512]{1,0:T(8,128)(2,1)}, bf16[512,512]{1,0:T(8,128)(2,1)}, u32[]{:S(2)}, u32[]{:S(2)}) collective-permute-start(bf16[512,512]{1,0:T(8,128)(2,1)} %get-tuple-element.17), channel_id=1, source_target_pairs={{0,4},{1,5},{2,6},{3,7},{4,0},{5,1},{6,2},{7,3},{8,12},{9,13},{10,... | collective-permute-start | bytes 1572872 | tf_op jit(solution)/shard_map/ppermute | solution.py:17
  14.8 4.9 %all-to-all-start = ((bf16[32,32,256]{2,1,0:T(8,128)(2,1)}), bf16[32,32,256]{2,1,0:T(8,128)(2,1)}, u32[]{:S(2)}, u32[]{:S(2)}) async-start(bf16[32,32,256]{2,1,0:T(8,128)(2,1)} %bitcast.12), calls=%async_computation | async-start | bytes 1048576 | tf_op jit(solution)/shard_map/all_to_all | solution.py:201
  20.9 9.6 %collective-permute-done.2.refs_3_ = bf16[512,512]{1,0:T(8,128)(2,1)S(1)} collective-permute-done((bf16[512,512]{1,0:T(8,128)(2,1)}, bf16[512,512]{1,0:T(8,128)(2,1)S(1)}, u32[]{:S(2)}, u32[]{:S(2)}) %collective-permute-start.2) | collective-permute-done | bytes 524320 | tf_op jit(solution)/shard_map/ppermute | solution.py:17
  30.6 3.0 %collective-permute-start.8 = (bf16[512,512]{1,0:T(8,128)(2,1)}, bf16[512,512]{1,0:T(8,128)(2,1)}, u32[]{:S(2)}, u32[]{:S(2)}) collective-permute-start(bf16[512,512]{1,0:T(8,128)(2,1)} %get-tuple-element.17), channel_id=1, source_target_pairs={{0,16},{1,17},{2,18},{3,19},{4,20},{5,21},{6,22},{7,23},{8,24},{9,... | collective-permute-start | bytes 1572872 | tf_op jit(solution)/shard_map/ppermute | solution.py:17
  33.6 14.4 %collective-permute-done.4.refs_5_.refs_1_ = bf16[512,512]{1,0:T(8,128)(2,1)} collective-permute-done((bf16[512,512]{1,0:T(8,128)(2,1)}, bf16[512,512]{1,0:T(8,128)(2,1)}, u32[]{:S(2)}, u32[]{:S(2)}) %collective-permute-start.4) | collective-permute-done | bytes 524320 | tf_op jit(solution)/shard_map/ppermute | solution.py:17
  47.9 2.7 %collective-permute-start.7 = (bf16[512,512]{1,0:T(8,128)(2,1)}, bf16[512,512]{1,0:T(8,128)(2,1)}, u32[]{:S(2)}, u32[]{:S(2)}) collective-permute-start(bf16[512,512]{1,0:T(8,128)(2,1)} %collective-permute-done.5.refs_6_.refs_2_), channel_id=1, source_target_pairs={{0,24},{1,25},{2,26},{3,27},{4,28},{5,29},{6,30},{7,31},{8,16},{9,... | collective-permute-start | bytes 1572872 | tf_op jit(solution)/shard_map/ppermute | solution.py:17
  52.6 5.5 %all-to-all-start.1 = ((bf16[32,32,256]{2,1,0:T(8,128)(2,1)}), bf16[32,32,256]{2,1,0:T(8,128)(2,1)S(1)}, u32[]{:S(2)}, u32[]{:S(2)}) async-start(bf16[32,32,256]{2,1,0:T(8,128)(2,1)} %copy-done.16), calls=%async_computation.1 | async-start | bytes 1048576 | tf_op jit(solution)/shard_map/all_to_all | solution.py:203
  58.1 13.4 %all-to-all-done.1 = bf16[32,32,256]{2,1,0:T(8,128)(2,1)S(1)} async-done(((bf16[32,32,256]{2,1,0:T(8,128)(2,1)}), bf16[32,32,256]{2,1,0:T(8,128)(2,1)S(1)}, u32[]{:S(2)}, u32[]{:S(2)}) %all-to-all-start.1) | async-done | bytes 524320 | tf_op jit(solution)/shard_map/all_to_all | solution.py:203
  78.6 7.4 %forward.1 = (bf16[1024,512]{1,0:T(8,128)(2,1)}, bf16[1024,512]{1,0:T(8,128)(2,1)S(1)}) custom-call(bf16[1024,256]{1,0:T(8,128)(2,1)S(1)} %bitcast.5, bf16[256,512]{1,0:T(8,128)(2,1)S(1)} %copy-done.17, bf16[1024,512]{1,0:T(8,128)(2,1)S(1)} %copy-done.20, bf16[512,3072]{1,0:T(8,128)(2,1)S(1)} %copy-done.2, bf16[1024,512]{1,0:T(8,128)(2,1)S(1)} %copy-done.1, ...), custom_call_target="tpu_custom_call" | custom-call | flops 1000 | bytes 1000 | tf_op jit(solution)/shard_map/forward/pallas_call | solution.py:36
  86.0 3.0 %give1.1 = bf16[1792,256]{1,0:T(8,128)(2,1)S(1)} custom-call(s32[1]{0:T(128)} %bitcast.4.core, bf16[1024,512]{1,0:T(8,128)(2,1)S(1)} %get-tuple-element.12.delta, bf16[512,512]{1,0:T(8,128)(2,1)} %collective-permute-done.3.refs_4_.refs_0_, bf16[512,512]{1,0:T(8,128)(2,1)} %collective-permute-done.4.refs_5_.refs_1_, ...), custom_call_target="tpu_custom_call" | custom-call | flops 1000 | bytes 1000 | tf_op jit(solution)/shard_map/give1/pallas_call | solution.py:36
  94.7 3.9 %back_yz.1 = (bf16[1024,512]{1,0:T(8,128)(2,1)}, bf16[1024,512]{1,0:T(8,128)(2,1)}, bf16[1024,512]{1,0:T(8,128)(2,1)}, bf16[1024,512]{1,0:T(8,128)(2,1)}) custom-call(bf16[1024,512]{1,0:T(8,128)(2,1)S(1)} %get-tuple-element.12.delta, bf16[512,3072]{1,0:T(8,128)(2,1)S(1)} %copy-done.3), custom_call_target="tpu_custom_call" | custom-call | flops 1000 | bytes 1000 | tf_op jit(solution)/shard_map/back_yz/pallas_call | solution.py:36
  103.0 6.3 %all-to-all-start.2 = ((bf16[32,32,256]{2,1,0:T(8,128)(2,1)}), bf16[32,32,256]{2,1,0:T(8,128)(2,1)}, u32[]{:S(2)}, u32[]{:S(2)}) async-start(bf16[32,32,256]{2,1,0:T(8,128)(2,1)} %bitcast.11), calls=%async_computation.2 | async-start | bytes 1048576 | tf_op jit(solution)/shard_map/all_to_all | solution.py:201
  111.5 4.0 %keep1.1.refs_0_ = bf16[1792,256]{1,0:T(8,128)(2,1)} custom-call(s32[1]{0:T(128)} %bitcast.4.core, bf16[1024,512]{1,0:T(8,128)(2,1)S(1)} %get-tuple-element.12.delta, bf16[1792,256]{1,0:T(8,128)(2,1)S(1)} %copy-done.22, bf16[512,512]{1,0:T(8,128)(2,1)} %collective-permute-done.3.refs_4_.refs_0_, bf16[512,512]{1,0:T(8,128)(2,1)} %collective-permute-done.4.refs_5_.refs_1_, ...), custom_call_target="tpu_custom_call" | custom-call | flops 1000 | bytes 1000 | tf_op jit(solution)/shard_map/keep1/pallas_call | solution.py:36
  115.5 2.5 %collective-permute-start.15 = (bf16[1792,256]{1,0:T(8,128)(2,1)}, bf16[1792,256]{1,0:T(8,128)(2,1)}, u32[]{:S(2)}, u32[]{:S(2)}) collective-permute-start(bf16[1792,256]{1,0:T(8,128)(2,1)} %keep1.1.refs_0_), channel_id=1, source_target_pairs={{0,64},{32,96},{64,0},{96,32},{1,65},{33,97},{65,1},{97,33},{2,66}... | collective-permute-start | bytes 2752520 | tf_op jit(solution)/shard_map/ppermute | solution.py:17
  118.0 3.0 %keep0.1.refs_0_ = bf16[1536,256]{1,0:T(8,128)(2,1)} custom-call(s32[1]{0:T(128)} %bitcast.4.core, bf16[1024,512]{1,0:T(8,128)(2,1)S(1)} %get-tuple-element.12.delta, bf16[1536,256]{1,0:T(8,128)(2,1)} %collective-permute-done.18.got, bf16[1024,512]{1,0:T(8,128)(2,1)S(1)} %copy-done.1, bf16[1024,512]{1,0:T(8,128)(2,1)S(1)} %collective-permute-done.refs_1_, ...), custom_call_target="tpu_custom_call" | custom-call | flops 1000 | bytes 1000 | tf_op jit(solution)/shard_map/keep0/pallas_call | solution.py:36
  121.6 5.6 %collective-permute-done.10.refs_1_ = bf16[1024,512]{1,0:T(8,128)(2,1)} collective-permute-done((bf16[1024,512]{1,0:T(8,128)(2,1)}, bf16[1024,512]{1,0:T(8,128)(2,1)}, u32[]{:S(2)}, u32[]{:S(2)}) %collective-permute-start.10) | collective-permute-done | bytes 1048608 | tf_op jit(solution)/shard_map/ppermute | solution.py:17
  128.7 24.7 %all-to-all-done.2.pieces = bf16[32,32,256]{2,1,0:T(8,128)(2,1)} async-done(((bf16[32,32,256]{2,1,0:T(8,128)(2,1)}), bf16[32,32,256]{2,1,0:T(8,128)(2,1)}, u32[]{:S(2)}, u32[]{:S(2)}) %all-to-all-start.2) | async-done | bytes 524320 | tf_op jit(solution)/shard_map/all_to_all | solution.py:201
  154.7 15.5 %all_to_all.20 = bf16[32,32,256]{2,1,0:T(8,128)(2,1)S(1)} all-to-all(bf16[32,32,256]{2,1,0:T(8,128)(2,1)S(1)} %back_sum.1), channel_id=1, replica_groups=mesh['dp'=4,'feat'=32] {'feat'}, dimensions={0} | all-to-all | bytes 1048576 | tf_op jit(solution)/shard_map/all_to_all | solution.py:203
  175.1 2.6 %collective-permute-start.23 = (bf16[512,128]{1,0:T(8,128)(2,1)S(1)}, bf16[512,128]{1,0:T(8,128)(2,1)S(1)}, u32[]{:S(2)}, u32[]{:S(2)}) collective-permute-start(bf16[512,128]{1,0:T(8,128)(2,1)S(1)} %keep_left.1.refs_0_), channel_id=1, source_target_pairs={{0,64},{32,96},{64,0},{96,32},{1,65},{33,97},{65,1},{97,33},{2,66}... | collective-permute-start | bytes 393224 | tf_op jit(solution)/shard_map/ppermute | solution.py:17
  177.7 3.7 %collective-permute-done.23.refs_1_ = bf16[512,128]{1,0:T(8,128)(2,1)S(1)} collective-permute-done((bf16[512,128]{1,0:T(8,128)(2,1)S(1)}, bf16[512,128]{1,0:T(8,128)(2,1)S(1)}, u32[]{:S(2)}, u32[]{:S(2)}) %collective-permute-start.23) | collective-permute-done | bytes 131104 | tf_op jit(solution)/shard_map/ppermute | solution.py:17
  183.9 5.0 %finish.1 = bf16[1024,512]{1,0:T(8,128)(2,1)} custom-call(bf16[1024,512]{1,0:T(8,128)(2,1)S(1)} %get-tuple-element.12.delta, bf16[512,3072]{1,0:T(8,128)(2,1)S(1)} %copy-done.4, bf16[1024,256]{1,0:T(8,128)(2,1)S(1)} %bitcast.10, bf16[512,256]{1,0:T(8,128)(2,1)S(1)} %copy-done.19, bf16[1024,512]{1,0:T(8,128)(2,1)} %collective-permute-done.9.refs_0_, ...), custom_call_target="tpu_custom_call" | custom-call | flops 1000 | bytes 1000 | tf_op jit(solution)/shard_map/finish/pallas_call | solution.py:36
  189.8 3.6 %put0.1.refs_4_ = f32[512,3072]{1,0:T(8,128)} custom-call(s32[1]{0:T(128)} %bitcast.4.core, bf16[1536,256]{1,0:T(8,128)(2,1)} %keep0.1.refs_0_, bf16[1536,256]{1,0:T(8,128)(2,1)} %collective-permute-done.19.refs_1_, bf16[1536,256]{1,0:T(8,128)(2,1)S(1)} %collective-permute-done.20.refs_2_, bf16[1536,256]{1,0:T(8,128)(2,1)S(1)} %collective-permute-done.21.refs_3_), custom_call_target="tpu_custom_call" | custom-call | flops 1000 | bytes 1000 | tf_op jit(solution)/shard_map/put0/pallas_call | solution.py:36
  195.3 3.7 %put1.1 = f32[512,3072]{1,0:T(8,128)} custom-call(s32[1]{0:T(128)} %bitcast.4.core, bf16[1792,256]{1,0:T(8,128)(2,1)} %keep1.1.refs_0_, bf16[1792,256]{1,0:T(8,128)(2,1)} %collective-permute-done.15.refs_1_, bf16[1792,256]{1,0:T(8,128)(2,1)S(1)} %collective-permute-done.16.refs_2_, ...), custom_call_target="tpu_custom_call", output_to_operand_aliasing={{}: (5, {})} | custom-call | flops 1000 | bytes 1000 | tf_op jit(solution)/shard_map/put1/pallas_call | solution.py:36
  (100 shorter events, 44.2 us)
Async XLA Ops:
  3.0 16.7 %collective-permute-start.1 = (bf16[512,512]{1,0:T(8,128)(2,1)}, bf16[512,512]{1,0:T(8,128)(2,1)S(1)}, u32[]{:S(2)}, u32[]{:S(2)}) collective-permute-start(bf16[512,512]{1,0:T(8,128)(2,1)} %get-tuple-element.18), channel_id=1, source_target_pairs={{0,2},{1,3},{2,0},{3,1},{4,6},{5,7},{6,4},{7,5},{8,10},{9,11},{10,... | collective-permute-start | bytes 1572872 | tf_op jit(solution)/shard_map/ppermute | solution.py:17
  5.5 25.1 %collective-permute-start.2 = (bf16[512,512]{1,0:T(8,128)(2,1)}, bf16[512,512]{1,0:T(8,128)(2,1)S(1)}, u32[]{:S(2)}, u32[]{:S(2)}) collective-permute-start(bf16[512,512]{1,0:T(8,128)(2,1)} %get-tuple-element.17), channel_id=1, source_target_pairs={{0,2},{1,3},{2,0},{3,1},{4,6},{5,7},{6,4},{7,5},{8,10},{9,11},{10,... | collective-permute-start | bytes 1572872 | tf_op jit(solution)/shard_map/ppermute | solution.py:17
  5.5 42.4 %collective-permute-start.4 = (bf16[512,512]{1,0:T(8,128)(2,1)}, bf16[512,512]{1,0:T(8,128)(2,1)}, u32[]{:S(2)}, u32[]{:S(2)}) collective-permute-start(bf16[512,512]{1,0:T(8,128)(2,1)} %get-tuple-element.17), channel_id=1, source_target_pairs={{0,4},{1,5},{2,6},{3,7},{4,0},{5,1},{6,2},{7,3},{8,12},{9,13},{10,... | collective-permute-start | bytes 1572872 | tf_op jit(solution)/shard_map/ppermute | solution.py:17
  8.9 63.5 %collective-permute-start = (bf16[1024,512]{1,0:T(8,128)(2,1)}, bf16[1024,512]{1,0:T(8,128)(2,1)S(1)}, u32[]{:S(2)}, u32[]{:S(2)}) collective-permute-start(bf16[1024,512]{1,0:T(8,128)(2,1)} %refs_0_.9), channel_id=1, source_target_pairs={{0,1},{1,0},{2,3},{3,2},{4,5},{5,4},{6,7},{7,6},{8,9},{9,8},{10,11... | collective-permute-start | bytes 3145736 | tf_op jit(solution)/shard_map/ppermute | solution.py:17
  10.1 37.8 %collective-permute-start.5 = (bf16[512,512]{1,0:T(8,128)(2,1)}, bf16[512,512]{1,0:T(8,128)(2,1)}, u32[]{:S(2)}, u32[]{:S(2)}) collective-permute-start(bf16[512,512]{1,0:T(8,128)(2,1)} %get-tuple-element.18), channel_id=1, source_target_pairs={{0,8},{1,9},{2,10},{3,11},{4,12},{5,13},{6,14},{7,15},{8,0},{9,1},... | collective-permute-start | bytes 1572872 | tf_op jit(solution)/shard_map/ppermute | solution.py:17
  14.8 35.9 %all-to-all-start = ((bf16[32,32,256]{2,1,0:T(8,128)(2,1)}), bf16[32,32,256]{2,1,0:T(8,128)(2,1)}, u32[]{:S(2)}, u32[]{:S(2)}) async-start(bf16[32,32,256]{2,1,0:T(8,128)(2,1)} %bitcast.12), calls=%async_computation | async-start | bytes 1048576 | tf_op jit(solution)/shard_map/all_to_all | solution.py:201
  19.7 38.4 %collective-permute-start.6 = (bf16[512,512]{1,0:T(8,128)(2,1)}, bf16[512,512]{1,0:T(8,128)(2,1)}, u32[]{:S(2)}, u32[]{:S(2)}) collective-permute-start(bf16[512,512]{1,0:T(8,128)(2,1)} %get-tuple-element.17), channel_id=1, source_target_pairs={{0,8},{1,9},{2,10},{3,11},{4,12},{5,13},{6,14},{7,15},{8,0},{9,1},... | collective-permute-start | bytes 1572872 | tf_op jit(solution)/shard_map/ppermute | solution.py:17
  30.6 27.6 %collective-permute-start.8 = (bf16[512,512]{1,0:T(8,128)(2,1)}, bf16[512,512]{1,0:T(8,128)(2,1)}, u32[]{:S(2)}, u32[]{:S(2)}) collective-permute-start(bf16[512,512]{1,0:T(8,128)(2,1)} %get-tuple-element.17), channel_id=1, source_target_pairs={{0,16},{1,17},{2,18},{3,19},{4,20},{5,21},{6,22},{7,23},{8,24},{9,... | collective-permute-start | bytes 1572872 | tf_op jit(solution)/shard_map/ppermute | solution.py:17
  47.9 24.4 %collective-permute-start.3 = (bf16[512,512]{1,0:T(8,128)(2,1)S(1)}, bf16[512,512]{1,0:T(8,128)(2,1)}, u32[]{:S(2)}, u32[]{:S(2)}) collective-permute-start(bf16[512,512]{1,0:T(8,128)(2,1)S(1)} %collective-permute-done.1.refs_2_), channel_id=1, source_target_pairs={{0,6},{1,7},{2,4},{3,5},{4,2},{5,3},{6,0},{7,1},{8,14},{9,15},{10,... | collective-permute-start | bytes 1572872 | tf_op jit(solution)/shard_map/ppermute | solution.py:17
  47.9 24.4 %collective-permute-start.7 = (bf16[512,512]{1,0:T(8,128)(2,1)}, bf16[512,512]{1,0:T(8,128)(2,1)}, u32[]{:S(2)}, u32[]{:S(2)}) collective-permute-start(bf16[512,512]{1,0:T(8,128)(2,1)} %collective-permute-done.5.refs_6_.refs_2_), channel_id=1, source_target_pairs={{0,24},{1,25},{2,26},{3,27},{4,28},{5,29},{6,30},{7,31},{8,16},{9,... | collective-permute-start | bytes 1572872 | tf_op jit(solution)/shard_map/ppermute | solution.py:17
  52.6 18.9 %all-to-all-start.1 = ((bf16[32,32,256]{2,1,0:T(8,128)(2,1)}), bf16[32,32,256]{2,1,0:T(8,128)(2,1)S(1)}, u32[]{:S(2)}, u32[]{:S(2)}) async-start(bf16[32,32,256]{2,1,0:T(8,128)(2,1)} %copy-done.16), calls=%async_computation.1 | async-start | bytes 1048576 | tf_op jit(solution)/shard_map/all_to_all | solution.py:203
  91.3 29.8 %collective-permute-start.9 = (bf16[1024,512]{1,0:T(8,128)(2,1)}, bf16[1024,512]{1,0:T(8,128)(2,1)}, u32[]{:S(2)}, u32[]{:S(2)}) collective-permute-start(bf16[1024,512]{1,0:T(8,128)(2,1)} %back_x.1), channel_id=1, source_target_pairs={{0,1},{1,0},{2,3},{3,2},{4,5},{5,4},{6,7},{7,6},{8,9},{9,8},{10,11... | collective-permute-start | bytes 3145736 | tf_op jit(solution)/shard_map/ppermute | solution.py:17
  94.2 21.3 %collective-permute-start.18 = (bf16[1536,256]{1,0:T(8,128)(2,1)}, bf16[1536,256]{1,0:T(8,128)(2,1)}, u32[]{:S(2)}, u32[]{:S(2)}) collective-permute-start(bf16[1536,256]{1,0:T(8,128)(2,1)} %give0.1), channel_id=1, source_target_pairs={{0,32},{32,0},{64,96},{96,64},{1,33},{33,1},{65,97},{97,65},{2,34}... | collective-permute-start | bytes 2359304 | tf_op jit(solution)/shard_map/ppermute | solution.py:17
  98.6 28.6 %collective-permute-start.10 = (bf16[1024,512]{1,0:T(8,128)(2,1)}, bf16[1024,512]{1,0:T(8,128)(2,1)}, u32[]{:S(2)}, u32[]{:S(2)}) collective-permute-start(bf16[1024,512]{1,0:T(8,128)(2,1)} %get-tuple-element.13), channel_id=1, source_target_pairs={{0,2},{1,3},{2,0},{3,1},{4,6},{5,7},{6,4},{7,5},{8,10},{9,11},{10,... | collective-permute-start | bytes 3145736 | tf_op jit(solution)/shard_map/ppermute | solution.py:17
  99.0 71.7 %collective-permute-start.11 = (bf16[1024,512]{1,0:T(8,128)(2,1)}, bf16[1024,512]{1,0:T(8,128)(2,1)}, u32[]{:S(2)}, u32[]{:S(2)}) collective-permute-start(bf16[1024,512]{1,0:T(8,128)(2,1)} %get-tuple-element.14), channel_id=1, source_target_pairs={{0,4},{1,5},{2,6},{3,7},{4,0},{5,1},{6,2},{7,3},{8,12},{9,13},{10,... | collective-permute-start | bytes 3145736 | tf_op jit(solution)/shard_map/ppermute | solution.py:17
  101.3 71.8 %collective-permute-start.12 = (bf16[1024,512]{1,0:T(8,128)(2,1)}, bf16[1024,512]{1,0:T(8,128)(2,1)}, u32[]{:S(2)}, u32[]{:S(2)}) collective-permute-start(bf16[1024,512]{1,0:T(8,128)(2,1)} %get-tuple-element.15), channel_id=1, source_target_pairs={{0,8},{1,9},{2,10},{3,11},{4,12},{5,13},{6,14},{7,15},{8,0},{9,1},... | collective-permute-start | bytes 3145736 | tf_op jit(solution)/shard_map/ppermute | solution.py:17
  103.0 50.4 %all-to-all-start.2 = ((bf16[32,32,256]{2,1,0:T(8,128)(2,1)}), bf16[32,32,256]{2,1,0:T(8,128)(2,1)}, u32[]{:S(2)}, u32[]{:S(2)}) async-start(bf16[32,32,256]{2,1,0:T(8,128)(2,1)} %bitcast.11), calls=%async_computation.2 | async-start | bytes 1048576 | tf_op jit(solution)/shard_map/all_to_all | solution.py:201
  115.5 57.7 %collective-permute-start.15 = (bf16[1792,256]{1,0:T(8,128)(2,1)}, bf16[1792,256]{1,0:T(8,128)(2,1)}, u32[]{:S(2)}, u32[]{:S(2)}) collective-permute-start(bf16[1792,256]{1,0:T(8,128)(2,1)} %keep1.1.refs_0_), channel_id=1, source_target_pairs={{0,64},{32,96},{64,0},{96,32},{1,65},{33,97},{65,1},{97,33},{2,66}... | collective-permute-start | bytes 2752520 | tf_op jit(solution)/shard_map/ppermute | solution.py:17
  121.0 53.4 %collective-permute-start.19 = (bf16[1536,256]{1,0:T(8,128)(2,1)}, bf16[1536,256]{1,0:T(8,128)(2,1)}, u32[]{:S(2)}, u32[]{:S(2)}) collective-permute-start(bf16[1536,256]{1,0:T(8,128)(2,1)} %keep0.1.refs_0_), channel_id=1, source_target_pairs={{0,64},{32,96},{64,0},{96,32},{1,65},{33,97},{65,1},{97,33},{2,66}... | collective-permute-start | bytes 2359304 | tf_op jit(solution)/shard_map/ppermute | solution.py:17
  127.2 47.9 %collective-permute-start.13 = (bf16[1024,512]{1,0:T(8,128)(2,1)}, bf16[1024,512]{1,0:T(8,128)(2,1)}, u32[]{:S(2)}, u32[]{:S(2)}) collective-permute-start(bf16[1024,512]{1,0:T(8,128)(2,1)} %get-tuple-element.16), channel_id=1, source_target_pairs={{0,16},{1,17},{2,18},{3,19},{4,20},{5,21},{6,22},{7,23},{8,24},{9,... | collective-permute-start | bytes 3145736 | tf_op jit(solution)/shard_map/ppermute | solution.py:17
  173.1 20.4 %collective-permute-start.16 = (bf16[1792,256]{1,0:T(8,128)(2,1)}, bf16[1792,256]{1,0:T(8,128)(2,1)S(1)}, u32[]{:S(2)}, u32[]{:S(2)}) collective-permute-start(bf16[1792,256]{1,0:T(8,128)(2,1)} %keep1.1.refs_0_), channel_id=1, source_target_pairs={{0,32},{32,0},{64,96},{96,64},{1,33},{33,1},{65,97},{97,65},{2,34}... | collective-permute-start | bytes 2752520 | tf_op jit(solution)/shard_map/ppermute | solution.py:17
  173.2 20.3 %collective-permute-start.17 = (bf16[1792,256]{1,0:T(8,128)(2,1)}, bf16[1792,256]{1,0:T(8,128)(2,1)S(1)}, u32[]{:S(2)}, u32[]{:S(2)}) collective-permute-start(bf16[1792,256]{1,0:T(8,128)(2,1)} %collective-permute-done.15.refs_1_), channel_id=1, source_target_pairs={{0,32},{32,0},{64,96},{96,64},{1,33},{33,1},{65,97},{97,65},{2,34}... | collective-permute-start | bytes 2752520 | tf_op jit(solution)/shard_map/ppermute | solution.py:17
  174.1 15.7 %collective-permute-start.20 = (bf16[1536,256]{1,0:T(8,128)(2,1)}, bf16[1536,256]{1,0:T(8,128)(2,1)S(1)}, u32[]{:S(2)}, u32[]{:S(2)}) collective-permute-start(bf16[1536,256]{1,0:T(8,128)(2,1)} %keep0.1.refs_0_), channel_id=1, source_target_pairs={{0,32},{32,0},{64,96},{96,64},{1,33},{33,1},{65,97},{97,65},{2,34}... | collective-permute-start | bytes 2359304 | tf_op jit(solution)/shard_map/ppermute | solution.py:17
  174.4 15.4 %collective-permute-start.21 = (bf16[1536,256]{1,0:T(8,128)(2,1)}, bf16[1536,256]{1,0:T(8,128)(2,1)S(1)}, u32[]{:S(2)}, u32[]{:S(2)}) collective-permute-start(bf16[1536,256]{1,0:T(8,128)(2,1)} %collective-permute-done.19.refs_1_), channel_id=1, source_target_pairs={{0,32},{32,0},{64,96},{96,64},{1,33},{33,1},{65,97},{97,65},{2,34}... | collective-permute-start | bytes 2359304 | tf_op jit(solution)/shard_map/ppermute | solution.py:17
  (28 other events, 385.3 us)

commit v3 on v0

v3 whole, which is shorter than its diff:
```python
import functools

import jax
import jax.numpy as jnp
from jax import lax
from jax.experimental import pallas as pl
from jax.experimental.pallas import tpu as pltpu
from jax.sharding import Mesh
from jax.sharding import PartitionSpec as P

BF = jnp.bfloat16
F32 = jnp.float32
TILE = 256
PLANE = ("y", "z")
SMEM = pl.BlockSpec(memory_space=pltpu.SMEM)
ANY = pl.BlockSpec(memory_space=pl.ANY)
WHOLE = pl.BlockSpec()


def flip(block, axis, mask):
    count = lax.axis_size(axis)
    return lax.ppermute(block, axis, [(i, i ^ mask) for i in range(count)])


def normal_cdf(value):
    return 0.5 * (1.0 + lax.erf(value * 0.7071067811865476))


def contract(first, second, first_dim, second_dim):
    return lax.dot_general(
        first, second, (((first_dim,), (second_dim,)), ((), ())), preferred_element_type=F32
    )


def struct(*shape_and_type):
    *shape, kind = shape_and_type
    return jax.ShapeDtypeStruct(tuple(shape), kind)


def call(kernel, outs, *args, name, vmem=24, after=(), specs=None, gflop=0.0, **more):
    specs = list(specs) if specs else [WHOLE] * len(args)

    def body(*refs):
        kernel(*refs[: len(args)], *refs[len(args) + len(after) :])

    return pl.pallas_call(
        body,
        out_shape=outs,
        name=name,
        in_specs=specs + [ANY] * len(after),
        compiler_params=pltpu.CompilerParams(vmem_limit_bytes=vmem << 20),
        cost_estimate=pl.CostEstimate(flops=1000 + int(gflop * 1e9), bytes_accessed=1000, transcendentals=0),
        **more,
    )(*args, *after)


def low_kernel(x, w, o):
    o[...] = jnp.dot(x[...], w[...], preferred_element_type=F32).astype(BF)


def halves_kernel(x, a, b):
    rows = a.shape[0]
    a[...] = x[:rows, :]
    b[...] = x[rows:, :]


def copy_kernel(*refs):
    count = len(refs) // 2
    for x, o in zip(refs[:count], refs[count:]):
        o[...] = x[...]


def hold(arrays, after, name):
    return call(copy_kernel, [struct(*a.shape, a.dtype) for a in arrays], *arrays, name=name, after=after)


def sum_kernel(pieces, total):
    acc = pieces[0].astype(F32)
    for k in range(1, pieces.shape[0]):
        acc = acc + pieces[k].astype(F32)
    total[...] = acc


def spread_kernel(mine, other, copies):
    total = (mine[...] + other[...]).astype(BF)
    for k in range(copies.shape[0]):
        copies[k] = total


def gather_rows(mine, name, after=()):
    count = lax.axis_size(PLANE)
    other = flip(mine, "xl", 1)
    copies = call(
        spread_kernel, struct(count, *mine.shape, BF), mine, other, name=name, after=after
    )
    return copies, lax.all_to_all(copies, PLANE, 0, 0).reshape(-1, mine.shape[1])


def scatter_rows(part):
    count = lax.axis_size(PLANE)
    return lax.all_to_all(part.reshape(count, -1, part.shape[1]), PLANE, 0, 0)


def row_sum(pieces, name, after=()):
    return call(sum_kernel, struct(*pieces.shape[1:], F32), pieces, name=name, after=after)


def forward_kernel(start, whole, reduced, right, cotangent, weight, *refs):
    blocks, (output, delta) = refs[:-2], refs[-2:]
    rows, bs = delta.shape
    for row in range(0, rows, TILE):
        here = slice(row, row + TILE)
        there = slice(start + row, start + row + TILE)
        pre = jnp.dot(reduced[there, :], right[...], preferred_element_type=F32)
        for slot, ref in enumerate(blocks):
            pre = pre + jnp.dot(
                ref[there if whole[slot] else here, :],
                weight[:, slot * bs : (slot + 1) * bs],
                preferred_element_type=F32,
            )
        cdf = normal_cdf(pre)
        output[here, :] = (pre * cdf).astype(BF)
        density = jnp.exp(-0.5 * pre * pre) * 0.3989422804014327
        delta[here, :] = (cotangent[there, :].astype(F32) * (cdf + pre * density)).astype(BF)


def slot_dots(slots, blocks, cols):
    out = []
    for parts in slots:
        total = None
        if len(parts) == len(cols):
            pairs = [(blocks[k][...], col) for k, col in zip(parts, cols)]
        else:
            step = cols[0].shape[0]
            pairs = [
                (blocks[parts[0]][n * step : (n + 1) * step, :], col) for n, col in enumerate(cols)
            ]
        for block, col in pairs:
            term = contract(block, col, 0, 0)
            total = term if total is None else total + term
        out.append(total)
    return out


def give_kernel(slots, n, core, *refs):
    deltas, blocks, out = refs[:n], refs[n:-1], refs[-1]
    hc = out.shape[1]

    def run(first):
        row = 0
        cols = [d[:, first : first + hc] for d in deltas]
        for total in slot_dots(sum(slots, ()), blocks, cols):
            out[row : row + total.shape[0], :] = total.astype(out.dtype)
            row += total.shape[0]

    pl.when(core[0] == 0)(lambda: run(hc))
    pl.when(core[0] == 1)(lambda: run(0))


def keep_kernel(slots, n, core, got, *refs):
    deltas, blocks, outs = refs[:n], refs[n : -len(slots)], refs[-len(slots) :]
    hc = got.shape[1]

    def run(first):
        start = 0
        cols = [d[:, first : first + hc] for d in deltas]
        for group, out in zip(slots, outs):
            row = 0
            for total in slot_dots(group, blocks, cols):
                size = total.shape[0]
                other = got[start : start + size, :].astype(F32)
                out[row : row + size, :] = (total + other).astype(out.dtype)
                row += size
                start += size

    pl.when(core[0] == 0)(lambda: run(0))
    pl.when(core[0] == 1)(lambda: run(hc))


def local_back_kernel(delta_a, delta_b, right, low):
    half = delta_a.shape[0]
    for first, delta in ((0, delta_a), (half, delta_b)):
        low[first : first + half, :] = contract(delta[...], right[...], 1, 1).astype(BF)


def back_kernel(slots, delta_a, delta_b, weight, *outs):
    half, bs = delta_a.shape
    for slot, out in zip(slots, outs):
        for first, delta in ((0, delta_a), (half, delta_b)):
            out[first : first + half, :] = contract(
                delta[...], weight[:, slot * bs : (slot + 1) * bs], 1, 1
            ).astype(BF)


def back_add_kernel(slot, delta_a, delta_b, weight, got, out):
    half, bs = delta_a.shape
    for first, delta in ((0, delta_a), (half, delta_b)):
        here = slice(first, first + half)
        term = contract(delta[...], weight[:, slot * bs : (slot + 1) * bs], 1, 1)
        out[here, :] = (term + got[here, :].astype(F32)).astype(BF)


def finish_kernel(delta_a, delta_b, weight, back_reduced, left, *refs):
    parts, out = refs[:-1], refs[-1]
    half, bs = delta_a.shape
    for first, delta in ((0, delta_a), (half, delta_b)):
        for row in range(0, half, TILE):
            here = slice(first + row, first + row + TILE)
            total = contract(delta[row : row + TILE, :], weight[:, :bs], 1, 1)
            total = total + contract(back_reduced[here, :], left[...], 1, 1)
            for part in parts:
                total = total + part[here, :].astype(F32)
            out[here, :] = total.astype(BF)


def assemble_kernel(with_old, core, *refs):
    mine, recv, mine_o, recv_o = refs[:4]
    out = refs[4 + with_old]

    def run(a, b, c, d):
        hc = a.shape[1]
        out[:, :hc] = a[...].astype(F32) + b[...].astype(F32)
        out[:, hc:] = c[...].astype(F32) + d[...].astype(F32)

    pl.when(core[0] == 0)(lambda: run(mine, recv, mine_o, recv_o))
    pl.when(core[0] == 1)(lambda: run(mine_o, recv_o, mine, recv))


def assemble(core, four, out, steps, in_start, out_start, old, name):
    hc = four[0].shape[1]
    bs = out.shape[0]
    half = pl.BlockSpec((bs, hc), lambda k: (k + in_start, 0))
    more = {}
    specs = [SMEM] + [half] * 4
    args = [core, *four]
    if old is not None:
        specs.append(pl.BlockSpec(memory_space=pl.ANY))
        args.append(old)
        more["input_output_aliases"] = {5: 0}
    return call(
        functools.partial(assemble_kernel, old is not None),
        out,
        *args,
        name=name,
        grid=(steps,),
        specs=specs,
        out_specs=pl.BlockSpec((bs, 2 * hc), lambda k: (0, k + out_start)),
        **more,
    )


def pick(slots, blocks):
    used = [k for group in slots for parts in group for k in parts]
    local = tuple(tuple(tuple(used.index(k) for k in parts) for parts in group) for group in slots)
    heights = [sum(blocks[parts[0]].shape[1] for parts in group) for group in slots]
    return local, [blocks[k] for k in used], heights


def give_half(core, slots, deltas, blocks, name, after=(), gflop=0.0):
    local, used, heights = pick(slots, blocks)
    n = len(deltas)
    give = call(
        functools.partial(give_kernel, local, n),
        [struct(sum(heights), deltas[0].shape[1] // 2, BF)],
        core,
        *deltas,
        *used,
        name="give_" + name,
        specs=[SMEM] + [WHOLE] * (n + len(used)),
        after=after,
        gflop=gflop,
    )
    return flip(give[0], "core", 1)


def keep_half(core, got, slots, deltas, blocks, name, after=(), gflop=0.0):
    local, used, heights = pick(slots, blocks)
    n = len(deltas)
    return call(
        functools.partial(keep_kernel, local, n),
        [struct(height, got.shape[1], BF) for height in heights],
        core,
        got,
        *deltas,
        *used,
        name="keep_" + name,
        specs=[SMEM] + [WHOLE] * (1 + n + len(used)),
        after=after,
        gflop=gflop,
    )


def over_chips(mine):
    recv = flip(mine, "xh", 1)
    return mine, recv, flip(mine, "core", 1), flip(recv, "core", 1)


def shards(tokens, butterfly, left_factor, right_factor, cotangent):
    rows, bs = tokens.shape
    rank = left_factor.shape[1]
    half = rows // 2
    core = lax.axis_index("core").astype(jnp.int32).reshape(1)

    t0 = flip(tokens, "xl", 1)
    first, second = call(halves_kernel, (struct(half, bs, BF),) * 2, tokens, name="halves")
    t1a, t3a = flip(first, "z", 1), flip(first, "y", 1)
    low = call(low_kernel, struct(rows, rank, BF), tokens, left_factor, name="low")
    low_mine = row_sum(scatter_rows(low), "low_sum", (t0, t1a, t3a))
    t1b, t3b = flip(second, "z", 1), flip(second, "y", 1)
    t2a, t4a = flip(t1a, "z", 3), flip(t3a, "y", 3)
    copies, reduced = gather_rows(low_mine, "low_spread")
    held = hold((t1b, t3b), (copies,), "hold_b")
    t2b, t4b = flip(held[0], "z", 3), flip(held[1], "y", 3)

    whole = (True, True, False, False, False, False)
    outs, deltas = [], []
    for start, parts, name in (
        (0, (t1a, t2a, t3a, t4a), "forward_a"),
        (half, (t1b, t2b, t3b, t4b), "forward_b"),
    ):
        out, delta = call(
            functools.partial(forward_kernel, start, whole),
            (struct(half, bs, BF), struct(half, bs, BF)),
            reduced,
            right_factor,
            cotangent,
            butterfly,
            tokens,
            t0,
            *parts,
            name=name,
            after=tuple(deltas),
            gflop=4.5,
        )
        outs.append(out)
        deltas.append(delta)
    output = jnp.concatenate(outs, axis=0)

    full = struct(rows, bs, BF)
    (c0,) = call(
        functools.partial(back_kernel, (1,)), (full,), *deltas, butterfly, name="back_x", gflop=1.0
    )
    r0 = flip(c0, "xl", 1)
    local_back = call(
        local_back_kernel,
        struct(rows, rank, BF),
        *deltas,
        right_factor,
        name="local_back",
        after=(c0,),
        gflop=0.5,
    )
    back_pieces = scatter_rows(local_back)
    blocks = (tokens, t0, t1a, t1b, t2a, t2b, t3a, t3b, t4a, t4b, reduced)
    slots = (((0,), (1,), (2, 3)), ((4, 5), (6, 7), (8, 9), (10,)))
    got = give_half(core, slots, deltas, blocks, "all", (local_back,), gflop=4.5)
    mine0, mine1 = keep_half(core, got, slots, deltas, blocks, "all", gflop=4.5)
    c2, c4 = call(
        functools.partial(back_kernel, (3, 5)),
        (full,) * 2,
        *deltas,
        butterfly,
        name="back_far",
        after=(back_pieces, mine0),
        gflop=2.0,
    )
    g2, g4 = flip(c2, "z", 3), flip(c4, "y", 3)
    back_mine = row_sum(back_pieces, "back_sum", (r0, c2))
    mine0, mine1 = hold((mine0, mine1), (back_mine,), "hold_halves")
    four0, four1 = over_chips(mine0), over_chips(mine1)
    copies, back_reduced = gather_rows(back_mine, "back_spread", (mine0, mine1))
    s1 = call(
        functools.partial(back_add_kernel, 2),
        full,
        *deltas,
        butterfly,
        g2,
        name="back_z",
        after=(copies,),
        gflop=2.0,
    )
    s3 = call(
        functools.partial(back_add_kernel, 4),
        full,
        *deltas,
        butterfly,
        g4,
        name="back_y",
        after=(copies,),
        gflop=2.0,
    )
    r1, r3 = flip(s1, "z", 1), flip(s3, "y", 1)
    left_slots = (((0,),),)
    left_got = give_half(core, left_slots, [back_reduced], blocks, "left", (s1, s3), gflop=0.5)
    (mine2,) = keep_half(core, left_got, left_slots, [back_reduced], blocks, "left", gflop=0.5)
    left_four = over_chips(mine2)

    grads = struct(*butterfly.shape, F32)
    grads_a = assemble(core, four0, grads, 3, 0, 0, None, "put0")
    grad_butterfly = assemble(core, four1, grads, 3, 0, 3, grads_a, "put1")
    grad_right = assemble(core, four1, struct(rank, bs, F32), 1, 3 * bs // rank, 0, None, "put_right")
    grad_left = assemble(core, left_four, struct(bs, rank, F32), 1, 0, 0, None, "put_left")

    grad_tokens = call(
        finish_kernel, full, *deltas, butterfly, back_reduced, left_factor, r0, r1, r3, name="finish"
    )
    return (output, grad_tokens, grad_butterfly, grad_left, grad_right)


def solution(mesh):
    axes = ("xh", "core", "y", "z", "xl")
    mesh = Mesh(mesh.devices.reshape(2, 2, 4, 4, 2), axes)
    dp, feat = axes[:2], axes[2:]
    in_specs = (P(dp, feat), P(feat, None), P(feat, None), P(None, feat), P(dp, feat))
    out_specs = (P(dp, feat), P(dp, feat), P(feat, None), P(feat, None), P(None, feat))
    return jax.shard_map(shards, mesh=mesh, in_specs=in_specs, out_specs=out_specs, check_vma=False)
```

time: 599 us -> 183 us (0.31)
  blocking collectives: 305 us -> 0 us
  waiting for transfers between devices: 212 us -> 30.5 us
  Pallas kernels: 0 us -> 51.2 us
  starting transfers between devices: 14.4 us -> 64.4 us
  matrix products: 43.5 us -> 0 us
  local copies, waits for them, and re-layouts: 8.61 us -> 31.7 us
  between operations: 14.3 us -> 0.93 us
    psum x2 -> x0, blocking collectives: 305 us -> none  [the longest x1 162 us: shards(): reduced = lax.psum(local_low, 'feat').astype(jnp.bfloat16)]
    psum x1 -> x0, waiting for transfers between devices: 168 us -> none  [shards(): lax.psum((grad_blocks, grad_left_local, grad_right_local), 'dp')]
    pallas_call x0 -> x24, Pallas kernels: none -> 51.2 us  [call(): pl.pallas_call(body, out_shape=outs, name=name, in_specs=specs + [ANY] *...]
    dot_general x24 -> x0, matrix products: 43.5 us -> none  [the longest x16 27.7 us: contract(): lax.dot_general(first, second, (((first_dim,), (second_dim,)), ((), ())),...]
    ppermute x10 -> x27, starting transfers between devices: 14.4 us -> 42.2 us  [flip(): return lax.ppermute(block, axis, [(i, i ^ mask) for i in range(count)])]
    ppermute x10 -> x27, waiting for transfers between devices: 43.6 us -> 20.2 us  [flip(): return lax.ppermute(block, axis, [(i, i ^ mask) for i in range(count)])]
    unnamed x21 -> x92, local copies, waits for them, and re-layouts: 8.61 us -> 31.7 us
    all_to_all x0 -> x4, starting transfers between devices: none -> 22.3 us  [the longest x2 11.5 us: scatter_rows(): return lax.all_to_all(part.reshape(count, -1, part.shape[1]), PLANE, 0, 0)]
  transfers between devices with their start and end apart: 11 -> 31, of which waited for: 4 -> 11; matrix products, arithmetic and copies ran while one was open for 3% -> 1% of each run, Pallas kernels for 0% -> 20%
where the time goes in v3:
time: 183 us; the launch traced here: 180 us
  starting transfers between devices  64.4 us (35%)
  Pallas kernels  51.2 us (28%)
  local copies, waits for them, and re-layouts  31.7 us (17%)
  waiting for transfers between devices  30.5 us (17%)
    pallas_call x24, Pallas kernels, call(): pl.pallas_call(body, out_shape=outs, name=name, in_specs=specs + [ANY] *...  51.2 us
    ppermute x27, starting transfers between devices, flip(): return lax.ppermute(block, axis, [(i, i ^ mask) for i in range(count)])  42.2 us
    unnamed x92, local copies, waits for them, and re-layouts  31.7 us
    ppermute x27, waiting for transfers between devices, flip(): return lax.ppermute(block, axis, [(i, i ^ mask) for i in range(count)])  20.2 us
    all_to_all x2, starting transfers between devices, scatter_rows(): return lax.all_to_all(part.reshape(count, -1, part.shape[1]), PLANE, 0, 0)  11.5 us
    all_to_all x2, starting transfers between devices, gather_rows(): lax.all_to_all(copies, PLANE, 0, 0).reshape(-1, mine.shape[1])  10.8 us
    all_to_all x2, waiting for transfers between devices, scatter_rows(): return lax.all_to_all(part.reshape(count, -1, part.shape[1]), PLANE, 0, 0)  8.13 us
  transfers between devices with their start and end apart: 31, of which 11 were waited for; matrix products, arithmetic and copies ran while one was open for 1% of the time, Pallas kernels for 20%

profile of v3, /device:TPU:1, one launch (start us, length us, event | category | flops | bytes accessed | tf_op | source)
XLA Modules:
  0.0 179.8 jit_solution(15904717445484224795)
XLA Ops:
  10.8 7.0 %all-to-all-start = ((bf16[16,64,256]{2,1,0:T(8,128)(2,1)}), bf16[16,64,256]{2,1,0:T(8,128)(2,1)S(1)}, u32[]{:S(2)}, u32[]{:S(2)}) async-start(bf16[16,64,256]{2,1,0:T(8,128)(2,1)} %bitcast), calls=%async_computation | async-start | bytes 1048576 | tf_op jit(solution)/shard_map/all_to_all | solution.py:101
  20.4 8.1 %all-to-all-done.refs_0_ = bf16[16,64,256]{2,1,0:T(8,128)(2,1)S(1)} async-done(((bf16[16,64,256]{2,1,0:T(8,128)(2,1)}), bf16[16,64,256]{2,1,0:T(8,128)(2,1)S(1)}, u32[]{:S(2)}, u32[]{:S(2)}) %all-to-all-start) | async-done | bytes 524320 | tf_op jit(solution)/shard_map/all_to_all | solution.py:101
  34.5 2.4 %collective-permute-start.4 = (bf16[512,512]{1,0:T(8,128)(2,1)}, bf16[512,512]{1,0:T(8,128)(2,1)}, u32[]{:S(2)}, u32[]{:S(2)}) collective-permute-start(bf16[512,512]{1,0:T(8,128)(2,1)} %collective-permute-done.1.refs_2_.refs_6_.refs_5_), channel_id=1, source_target_pairs={{0,6},{2,4},{4,2},{6,0},{1,7},{3,5},{5,3},{7,1},{8,14},{10,12},{12... | collective-permute-start | bytes 1572872 | tf_op jit(solution)/shard_map/ppermute | solution.py:22
  37.7 4.3 %all-to-all-start.1 = ((bf16[16,64,256]{2,1,0:T(8,128)(2,1)}), bf16[16,64,256]{2,1,0:T(8,128)(2,1)}, u32[]{:S(2)}, u32[]{:S(2)}) async-start(bf16[16,64,256]{2,1,0:T(8,128)(2,1)} %copy-done.16), calls=%async_computation.1 | async-start | bytes 1048576 | tf_op jit(solution)/shard_map/all_to_all | solution.py:96
  47.7 2.5 %collective-permute-start.9 = (bf16[512,512]{1,0:T(8,128)(2,1)}, bf16[512,512]{1,0:T(8,128)(2,1)}, u32[]{:S(2)}, u32[]{:S(2)}) collective-permute-start(bf16[512,512]{1,0:T(8,128)(2,1)} %get-tuple-element.23), channel_id=1, source_target_pairs={{0,24},{8,16},{16,8},{24,0},{1,25},{9,17},{17,9},{25,1},{2,26},{10... | collective-permute-start | bytes 1572872 | tf_op jit(solution)/shard_map/ppermute | solution.py:22
  56.0 4.0 %forward_a.1 = (bf16[512,512]{1,0:T(8,128)(2,1)S(1)}, bf16[512,512]{1,0:T(8,128)(2,1)S(1)}) custom-call(bf16[1024,256]{1,0:T(8,128)(2,1)} %bitcast.1.refs_0_.refs_13_.refs_14_, bf16[256,512]{1,0:T(8,128)(2,1)S(1)} %copy-done.43, bf16[1024,512]{1,0:T(8,128)(2,1)S(1)} %copy-done.44, bf16[512,3072]{1,0:T(8,128)(2,1)S(1)} %copy-done, ...), custom_call_target="tpu_custom_call" | custom-call | flops 4500000768 | bytes 1000 | tf_op jit(solution)/shard_map/forward_a/pallas_call | solution.py:46
  60.8 3.7 %collective-permute-done.8.refs_7_.refs_8_.refs_9_ = bf16[512,512]{1,0:T(8,128)(2,1)} collective-permute-done((bf16[512,512]{1,0:T(8,128)(2,1)}, bf16[512,512]{1,0:T(8,128)(2,1)}, u32[]{:S(2)}, u32[]{:S(2)}) %collective-permute-start.8) | collective-permute-done | bytes 524320 | tf_op jit(solution)/shard_map/ppermute | solution.py:22
  64.5 4.0 %forward_b.1 = (bf16[512,512]{1,0:T(8,128)(2,1)S(1)}, bf16[512,512]{1,0:T(8,128)(2,1)S(1)}) custom-call(bf16[1024,256]{1,0:T(8,128)(2,1)} %bitcast.1.refs_0_.refs_13_.refs_14_, bf16[256,512]{1,0:T(8,128)(2,1)S(1)} %copy-done.43, bf16[1024,512]{1,0:T(8,128)(2,1)S(1)} %copy-done.44, bf16[512,3072]{1,0:T(8,128)(2,1)S(1)} %copy-done, ...), custom_call_target="tpu_custom_call" | custom-call | flops 4500000768 | bytes 1000 | tf_op jit(solution)/shard_map/forward_b/pallas_call | solution.py:46
  71.2 5.5 %give_all.1 = bf16[3328,256]{1,0:T(8,128)(2,1)} custom-call(s32[1]{0:T(128)} %bitcast.3.refs_0_, bf16[512,512]{1,0:T(8,128)(2,1)S(1)} %get-tuple-element.24.refs_10_.refs_0_.refs_1_.refs_2_, bf16[512,512]{1,0:T(8,128)(2,1)S(1)} %get-tuple-element.26.refs_1_.refs_2_.refs_3_, bf16[1024,512]{1,0:T(8,128)(2,1)S(1)} %copy-done.3, ...), custom_call_target="tpu_custom_call" | custom-call | flops 4500000768 | bytes 1000 | tf_op jit(solution)/shard_map/give_all/pallas_call | solution.py:46
  76.6 2.9 %collective-permute-start.11 = (bf16[3328,256]{1,0:T(8,128)(2,1)}, bf16[3328,256]{1,0:T(8,128)(2,1)}, u32[]{:S(2)}, u32[]{:S(2)}) collective-permute-start(bf16[3328,256]{1,0:T(8,128)(2,1)} %give_all.1), channel_id=1, source_target_pairs={{0,32},{32,0},{1,33},{33,1},{2,34},{34,2},{3,35},{35,3},{4,36},{36... | collective-permute-start | bytes 5111816 | tf_op jit(solution)/shard_map/ppermute | solution.py:22
  79.5 4.5 %all-to-all-start.2 = ((bf16[16,64,256]{2,1,0:T(8,128)(2,1)}), bf16[16,64,256]{2,1,0:T(8,128)(2,1)}, u32[]{:S(2)}, u32[]{:S(2)}) async-start(bf16[16,64,256]{2,1,0:T(8,128)(2,1)} %bitcast.5), calls=%async_computation.2 | async-start | bytes 1048576 | tf_op jit(solution)/shard_map/all_to_all | solution.py:101
  89.7 4.8 %keep_all.1 = (bf16[1536,256]{1,0:T(8,128)(2,1)S(1)}, bf16[1792,256]{1,0:T(8,128)(2,1)S(1)}) custom-call(s32[1]{0:T(128)} %bitcast.3.refs_0_, bf16[3328,256]{1,0:T(8,128)(2,1)} %collective-permute-done.11.refs_1_, bf16[512,512]{1,0:T(8,128)(2,1)S(1)} %copy-done.7, bf16[512,512]{1,0:T(8,128)(2,1)S(1)} %copy-done.12, bf16[1024,512]{1,0:T(8,128)(2,1)S(1)} %copy-done.4, ...), custom_call_target="tpu_custom_call" | custom-call | flops 4500000768 | bytes 1000 | tf_op jit(solution)/shard_map/keep_all/pallas_call | solution.py:46
  99.6 2.5 %back_far.1 = (bf16[1024,512]{1,0:T(8,128)(2,1)}, bf16[1024,512]{1,0:T(8,128)(2,1)}) custom-call(bf16[512,512]{1,0:T(8,128)(2,1)S(1)} %copy-done.8, bf16[512,512]{1,0:T(8,128)(2,1)S(1)} %copy-done.13, bf16[512,3072]{1,0:T(8,128)(2,1)S(1)} %copy-done, bf16[16,64,256]{2,1,0:T(8,128)(2,1)} %all-to-all-done.2.refs_3_.refs_0_, bf16[1536,256]{1,0:T(8,128)(2,1)S(1)} %copy-done.37), custom_call_target="tpu_custom_call" | custom-call | flops 2000001024 | bytes 1000 | tf_op jit(solution)/shard_map/back_far/pallas_call | solution.py:46
  104.5 2.4 %collective-permute-start.13 = (bf16[1024,512]{1,0:T(8,128)(2,1)}, bf16[1024,512]{1,0:T(8,128)(2,1)}, u32[]{:S(2)}, u32[]{:S(2)}) collective-permute-start(bf16[1024,512]{1,0:T(8,128)(2,1)} %get-tuple-element.28.refs_2_), channel_id=1, source_target_pairs={{0,6},{2,4},{4,2},{6,0},{1,7},{3,5},{5,3},{7,1},{8,14},{10,12},{12... | collective-permute-start | bytes 3145736 | tf_op jit(solution)/shard_map/ppermute | solution.py:22
  112.8 2.4 %collective-permute-start.17 = (bf16[1792,256]{1,0:T(8,128)(2,1)}, bf16[1792,256]{1,0:T(8,128)(2,1)}, u32[]{:S(2)}, u32[]{:S(2)}) collective-permute-start(bf16[1792,256]{1,0:T(8,128)(2,1)} %get-tuple-element.31.refs_3_.refs_1_), channel_id=1, source_target_pairs={{0,64},{64,0},{1,65},{65,1},{2,66},{66,2},{3,67},{67,3},{4,68},{68... | collective-permute-start | bytes 2752520 | tf_op jit(solution)/shard_map/ppermute | solution.py:22
  118.0 6.5 %all-to-all-start.3 = ((bf16[16,64,256]{2,1,0:T(8,128)(2,1)}), bf16[16,64,256]{2,1,0:T(8,128)(2,1)}, u32[]{:S(2)}, u32[]{:S(2)}) async-start(bf16[16,64,256]{2,1,0:T(8,128)(2,1)} %copy-done.22), calls=%async_computation.3 | async-start | bytes 1048576 | tf_op jit(solution)/shard_map/all_to_all | solution.py:96
  124.5 3.6 %collective-permute-done.15.refs_3_ = bf16[1024,512]{1,0:T(8,128)(2,1)} collective-permute-done((bf16[1024,512]{1,0:T(8,128)(2,1)}, bf16[1024,512]{1,0:T(8,128)(2,1)}, u32[]{:S(2)}, u32[]{:S(2)}) %collective-permute-start.15) | collective-permute-done | bytes 1048608 | tf_op jit(solution)/shard_map/ppermute | solution.py:22
  131.2 3.0 %back_y.1.refs_4_ = bf16[1024,512]{1,0:T(8,128)(2,1)} custom-call(bf16[512,512]{1,0:T(8,128)(2,1)S(1)} %copy-done.9, bf16[512,512]{1,0:T(8,128)(2,1)S(1)} %copy-done.14, bf16[512,3072]{1,0:T(8,128)(2,1)S(1)} %copy-done, bf16[1024,512]{1,0:T(8,128)(2,1)} %collective-permute-done.15.refs_3_, bf16[16,64,256]{2,1,0:T(8,128)(2,1)S(1)} %copy-done.23), custom_call_target="tpu_custom_call" | custom-call | flops 2000001024 | bytes 1000 | tf_op jit(solution)/shard_map/back_y/pallas_call | solution.py:46
  141.3 4.1 %collective-permute-start.23 = (bf16[512,128]{1,0:T(8,128)(2,1)S(1)}, bf16[512,128]{1,0:T(8,128)(2,1)S(1)}, u32[]{:S(2)}, u32[]{:S(2)}) collective-permute-start(bf16[512,128]{1,0:T(8,128)(2,1)S(1)} %give_left.1), channel_id=1, source_target_pairs={{0,32},{32,0},{1,33},{33,1},{2,34},{34,2},{3,35},{35,3},{4,36},{36... | collective-permute-start | bytes 393224 | tf_op jit(solution)/shard_map/ppermute | solution.py:22
  147.9 2.5 %collective-permute-start.24 = (bf16[512,128]{1,0:T(8,128)(2,1)S(1)}, bf16[512,128]{1,0:T(8,128)(2,1)S(1)}, u32[]{:S(2)}, u32[]{:S(2)}) collective-permute-start(bf16[512,128]{1,0:T(8,128)(2,1)S(1)} %keep_left.1.refs_1_), channel_id=1, source_target_pairs={{0,64},{64,0},{1,65},{65,1},{2,66},{66,2},{3,67},{67,3},{4,68},{68... | collective-permute-start | bytes 393224 | tf_op jit(solution)/shard_map/ppermute | solution.py:22
  162.0 4.1 %put0.1.refs_5_ = f32[512,3072]{1,0:T(8,128)} custom-call(s32[1]{0:T(128)} %bitcast.3.refs_0_, bf16[1536,256]{1,0:T(8,128)(2,1)} %get-tuple-element.30.refs_2_.refs_1_, bf16[1536,256]{1,0:T(8,128)(2,1)} %collective-permute-done.20.refs_2_, bf16[1536,256]{1,0:T(8,128)(2,1)} %collective-permute-done.21.refs_3_, ...), custom_call_target="tpu_custom_call" | custom-call | flops 1000 | bytes 1000 | tf_op jit(solution)/shard_map/put0/pallas_call | solution.py:46
  167.9 3.8 %put1.1 = f32[512,3072]{1,0:T(8,128)} custom-call(s32[1]{0:T(128)} %bitcast.3.refs_0_, bf16[1792,256]{1,0:T(8,128)(2,1)} %get-tuple-element.31.refs_3_.refs_1_, bf16[1792,256]{1,0:T(8,128)(2,1)} %collective-permute-done.17.refs_2_, bf16[1792,256]{1,0:T(8,128)(2,1)S(1)} %collective-permute-done.18.refs_3_, ...), custom_call_target="tpu_custom_call", output_to_operand_aliasing={{}: (5, {})} | custom-call | flops 1000 | bytes 1000 | tf_op jit(solution)/shard_map/put1/pallas_call | solution.py:46
  171.7 4.4 %collective-permute-done.16.refs_7_ = bf16[1024,512]{1,0:T(8,128)(2,1)S(1)} collective-permute-done((bf16[1024,512]{1,0:T(8,128)(2,1)}, bf16[1024,512]{1,0:T(8,128)(2,1)S(1)}, u32[]{:S(2)}, u32[]{:S(2)}) %collective-permute-start.16) | collective-permute-done | bytes 1048608 | tf_op jit(solution)/shard_map/ppermute | solution.py:22
  176.1 3.7 %finish.1 = bf16[1024,512]{1,0:T(8,128)(2,1)} custom-call(bf16[512,512]{1,0:T(8,128)(2,1)S(1)} %copy-done.10, bf16[512,512]{1,0:T(8,128)(2,1)S(1)} %copy-done.15, bf16[512,3072]{1,0:T(8,128)(2,1)S(1)} %copy-done, bf16[1024,256]{1,0:T(8,128)(2,1)} %bitcast.4.refs_3_.refs_1_.refs_2_, bf16[512,256]{1,0:T(8,128)(2,1)S(1)} %copy-done.25, ...), custom_call_target="tpu_custom_call" | custom-call | flops 1000 | bytes 1000 | tf_op jit(solution)/shard_map/finish/pallas_call | solution.py:46
  (155 shorter events, 82.3 us)
Async XLA Ops:
  0.6 28.7 %collective-permute-start = (bf16[1024,512]{1,0:T(8,128)(2,1)}, bf16[1024,512]{1,0:T(8,128)(2,1)S(1)}, u32[]{:S(2)}, u32[]{:S(2)}) collective-permute-start(bf16[1024,512]{1,0:T(8,128)(2,1)} %refs_3_.7), channel_id=1, source_target_pairs={{0,1},{1,0},{2,3},{3,2},{4,5},{5,4},{6,7},{7,6},{8,9},{9,8},{10,11... | collective-permute-start | bytes 3145736 | tf_op jit(solution)/shard_map/ppermute | solution.py:22
  5.7 23.6 %collective-permute-start.2 = (bf16[512,512]{1,0:T(8,128)(2,1)}, bf16[512,512]{1,0:T(8,128)(2,1)}, u32[]{:S(2)}, u32[]{:S(2)}) collective-permute-start(bf16[512,512]{1,0:T(8,128)(2,1)} %get-tuple-element.19), channel_id=1, source_target_pairs={{0,8},{8,0},{16,24},{24,16},{1,9},{9,1},{17,25},{25,17},{2,10},{10... | collective-permute-start | bytes 1572872 | tf_op jit(solution)/shard_map/ppermute | solution.py:22
  7.0 22.3 %collective-permute-start.1 = (bf16[512,512]{1,0:T(8,128)(2,1)}, bf16[512,512]{1,0:T(8,128)(2,1)}, u32[]{:S(2)}, u32[]{:S(2)}) collective-permute-start(bf16[512,512]{1,0:T(8,128)(2,1)} %get-tuple-element.19), channel_id=1, source_target_pairs={{0,2},{2,0},{4,6},{6,4},{1,3},{3,1},{5,7},{7,5},{8,10},{10,8},{12,... | collective-permute-start | bytes 1572872 | tf_op jit(solution)/shard_map/ppermute | solution.py:22
  10.8 17.7 %all-to-all-start = ((bf16[16,64,256]{2,1,0:T(8,128)(2,1)}), bf16[16,64,256]{2,1,0:T(8,128)(2,1)S(1)}, u32[]{:S(2)}, u32[]{:S(2)}) async-start(bf16[16,64,256]{2,1,0:T(8,128)(2,1)} %bitcast), calls=%async_computation | async-start | bytes 1048576 | tf_op jit(solution)/shard_map/all_to_all | solution.py:101
  17.8 24.2 %collective-permute-start.7 = (bf16[512,512]{1,0:T(8,128)(2,1)}, bf16[512,512]{1,0:T(8,128)(2,1)}, u32[]{:S(2)}, u32[]{:S(2)}) collective-permute-start(bf16[512,512]{1,0:T(8,128)(2,1)} %copy-done.45), channel_id=1, source_target_pairs={{0,8},{8,0},{16,24},{24,16},{1,9},{9,1},{17,25},{25,17},{2,10},{10... | collective-permute-start | bytes 1572872 | tf_op jit(solution)/shard_map/ppermute | solution.py:22
  19.2 22.8 %collective-permute-start.6 = (bf16[512,512]{1,0:T(8,128)(2,1)}, bf16[512,512]{1,0:T(8,128)(2,1)}, u32[]{:S(2)}, u32[]{:S(2)}) collective-permute-start(bf16[512,512]{1,0:T(8,128)(2,1)} %copy-done.45), channel_id=1, source_target_pairs={{0,2},{2,0},{4,6},{6,4},{1,3},{3,1},{5,7},{7,5},{8,10},{10,8},{12,... | collective-permute-start | bytes 1572872 | tf_op jit(solution)/shard_map/ppermute | solution.py:22
  33.0 17.2 %collective-permute-start.5 = (bf16[512,512]{1,0:T(8,128)(2,1)}, bf16[512,512]{1,0:T(8,128)(2,1)}, u32[]{:S(2)}, u32[]{:S(2)}) collective-permute-start(bf16[512,512]{1,0:T(8,128)(2,1)} %collective-permute-done.2.refs_3_.refs_8_.refs_9_.refs_10_), channel_id=1, source_target_pairs={{0,24},{8,16},{16,8},{24,0},{1,25},{9,17},{17,9},{25,1},{2,26},{10... | collective-permute-start | bytes 1572872 | tf_op jit(solution)/shard_map/ppermute | solution.py:22
  34.5 15.7 %collective-permute-start.4 = (bf16[512,512]{1,0:T(8,128)(2,1)}, bf16[512,512]{1,0:T(8,128)(2,1)}, u32[]{:S(2)}, u32[]{:S(2)}) collective-permute-start(bf16[512,512]{1,0:T(8,128)(2,1)} %collective-permute-done.1.refs_2_.refs_6_.refs_5_), channel_id=1, source_target_pairs={{0,6},{2,4},{4,2},{6,0},{1,7},{3,5},{5,3},{7,1},{8,14},{10,12},{12... | collective-permute-start | bytes 1572872 | tf_op jit(solution)/shard_map/ppermute | solution.py:22
  37.7 14.6 %all-to-all-start.1 = ((bf16[16,64,256]{2,1,0:T(8,128)(2,1)}), bf16[16,64,256]{2,1,0:T(8,128)(2,1)}, u32[]{:S(2)}, u32[]{:S(2)}) async-start(bf16[16,64,256]{2,1,0:T(8,128)(2,1)} %copy-done.16), calls=%async_computation.1 | async-start | bytes 1048576 | tf_op jit(solution)/shard_map/all_to_all | solution.py:96
  45.3 19.2 %collective-permute-start.8 = (bf16[512,512]{1,0:T(8,128)(2,1)}, bf16[512,512]{1,0:T(8,128)(2,1)}, u32[]{:S(2)}, u32[]{:S(2)}) collective-permute-start(bf16[512,512]{1,0:T(8,128)(2,1)} %get-tuple-element.22), channel_id=1, source_target_pairs={{0,6},{2,4},{4,2},{6,0},{1,7},{3,5},{5,3},{7,1},{8,14},{10,12},{12... | collective-permute-start | bytes 1572872 | tf_op jit(solution)/shard_map/ppermute | solution.py:22
  47.7 16.8 %collective-permute-start.9 = (bf16[512,512]{1,0:T(8,128)(2,1)}, bf16[512,512]{1,0:T(8,128)(2,1)}, u32[]{:S(2)}, u32[]{:S(2)}) collective-permute-start(bf16[512,512]{1,0:T(8,128)(2,1)} %get-tuple-element.23), channel_id=1, source_target_pairs={{0,24},{8,16},{16,8},{24,0},{1,25},{9,17},{17,9},{25,1},{2,26},{10... | collective-permute-start | bytes 1572872 | tf_op jit(solution)/shard_map/ppermute | solution.py:22
  76.6 8.5 %collective-permute-start.11 = (bf16[3328,256]{1,0:T(8,128)(2,1)}, bf16[3328,256]{1,0:T(8,128)(2,1)}, u32[]{:S(2)}, u32[]{:S(2)}) collective-permute-start(bf16[3328,256]{1,0:T(8,128)(2,1)} %give_all.1), channel_id=1, source_target_pairs={{0,32},{32,0},{1,33},{33,1},{2,34},{34,2},{3,35},{35,3},{4,36},{36... | collective-permute-start | bytes 5111816 | tf_op jit(solution)/shard_map/ppermute | solution.py:22
  79.5 16.9 %all-to-all-start.2 = ((bf16[16,64,256]{2,1,0:T(8,128)(2,1)}), bf16[16,64,256]{2,1,0:T(8,128)(2,1)}, u32[]{:S(2)}, u32[]{:S(2)}) async-start(bf16[16,64,256]{2,1,0:T(8,128)(2,1)} %bitcast.5), calls=%async_computation.2 | async-start | bytes 1048576 | tf_op jit(solution)/shard_map/all_to_all | solution.py:101
  84.0 24.9 %collective-permute-start.10 = (bf16[1024,512]{1,0:T(8,128)(2,1)}, bf16[1024,512]{1,0:T(8,128)(2,1)}, u32[]{:S(2)}, u32[]{:S(2)}) collective-permute-start(bf16[1024,512]{1,0:T(8,128)(2,1)} %copy-done.18), channel_id=1, source_target_pairs={{0,1},{1,0},{2,3},{3,2},{4,5},{5,4},{6,7},{7,6},{8,9},{9,8},{10,11... | collective-permute-start | bytes 3145736 | tf_op jit(solution)/shard_map/ppermute | solution.py:22
  102.1 26.0 %collective-permute-start.15 = (bf16[1024,512]{1,0:T(8,128)(2,1)}, bf16[1024,512]{1,0:T(8,128)(2,1)}, u32[]{:S(2)}, u32[]{:S(2)}) collective-permute-start(bf16[1024,512]{1,0:T(8,128)(2,1)} %get-tuple-element.32), channel_id=1, source_target_pairs={{0,24},{8,16},{16,8},{24,0},{1,25},{9,17},{17,9},{25,1},{2,26},{10... | collective-permute-start | bytes 3145736 | tf_op jit(solution)/shard_map/ppermute | solution.py:22
  104.5 29.8 %collective-permute-start.13 = (bf16[1024,512]{1,0:T(8,128)(2,1)}, bf16[1024,512]{1,0:T(8,128)(2,1)}, u32[]{:S(2)}, u32[]{:S(2)}) collective-permute-start(bf16[1024,512]{1,0:T(8,128)(2,1)} %get-tuple-element.28.refs_2_), channel_id=1, source_target_pairs={{0,6},{2,4},{4,2},{6,0},{1,7},{3,5},{5,3},{7,1},{8,14},{10,12},{12... | collective-permute-start | bytes 3145736 | tf_op jit(solution)/shard_map/ppermute | solution.py:22
  112.8 44.1 %collective-permute-start.17 = (bf16[1792,256]{1,0:T(8,128)(2,1)}, bf16[1792,256]{1,0:T(8,128)(2,1)}, u32[]{:S(2)}, u32[]{:S(2)}) collective-permute-start(bf16[1792,256]{1,0:T(8,128)(2,1)} %get-tuple-element.31.refs_3_.refs_1_), channel_id=1, source_target_pairs={{0,64},{64,0},{1,65},{65,1},{2,66},{66,2},{3,67},{67,3},{4,68},{68... | collective-permute-start | bytes 2752520 | tf_op jit(solution)/shard_map/ppermute | solution.py:22
  115.2 35.9 %collective-permute-start.21 = (bf16[1536,256]{1,0:T(8,128)(2,1)}, bf16[1536,256]{1,0:T(8,128)(2,1)}, u32[]{:S(2)}, u32[]{:S(2)}) collective-permute-start(bf16[1536,256]{1,0:T(8,128)(2,1)} %get-tuple-element.30.refs_2_.refs_1_), channel_id=1, source_target_pairs={{0,32},{32,0},{1,33},{33,1},{2,34},{34,2},{3,35},{35,3},{4,36},{36... | collective-permute-start | bytes 2359304 | tf_op jit(solution)/shard_map/ppermute | solution.py:22
  116.6 35.6 %collective-permute-start.20 = (bf16[1536,256]{1,0:T(8,128)(2,1)}, bf16[1536,256]{1,0:T(8,128)(2,1)}, u32[]{:S(2)}, u32[]{:S(2)}) collective-permute-start(bf16[1536,256]{1,0:T(8,128)(2,1)} %get-tuple-element.30.refs_2_.refs_1_), channel_id=1, source_target_pairs={{0,64},{64,0},{1,65},{65,1},{2,66},{66,2},{3,67},{67,3},{4,68},{68... | collective-permute-start | bytes 2359304 | tf_op jit(solution)/shard_map/ppermute | solution.py:22
  118.0 19.2 %all-to-all-start.3 = ((bf16[16,64,256]{2,1,0:T(8,128)(2,1)}), bf16[16,64,256]{2,1,0:T(8,128)(2,1)}, u32[]{:S(2)}, u32[]{:S(2)}) async-start(bf16[16,64,256]{2,1,0:T(8,128)(2,1)} %copy-done.22), calls=%async_computation.3 | async-start | bytes 1048576 | tf_op jit(solution)/shard_map/all_to_all | solution.py:96
  151.1 25.0 %collective-permute-start.16 = (bf16[1024,512]{1,0:T(8,128)(2,1)}, bf16[1024,512]{1,0:T(8,128)(2,1)S(1)}, u32[]{:S(2)}, u32[]{:S(2)}) collective-permute-start(bf16[1024,512]{1,0:T(8,128)(2,1)} %back_y.1.refs_4_), channel_id=1, source_target_pairs={{0,8},{8,0},{16,24},{24,16},{1,9},{9,1},{17,25},{25,17},{2,10},{10... | collective-permute-start | bytes 3145736 | tf_op jit(solution)/shard_map/ppermute | solution.py:22
  152.2 23.9 %collective-permute-start.14 = (bf16[1024,512]{1,0:T(8,128)(2,1)S(1)}, bf16[1024,512]{1,0:T(8,128)(2,1)S(1)}, u32[]{:S(2)}, u32[]{:S(2)}) collective-permute-start(bf16[1024,512]{1,0:T(8,128)(2,1)S(1)} %copy-done.33), channel_id=1, source_target_pairs={{0,2},{2,0},{4,6},{6,4},{1,3},{3,1},{5,7},{7,5},{8,10},{10,8},{12,... | collective-permute-start | bytes 3145736 | tf_op jit(solution)/shard_map/ppermute | solution.py:22
  156.9 9.2 %collective-permute-start.18 = (bf16[1792,256]{1,0:T(8,128)(2,1)}, bf16[1792,256]{1,0:T(8,128)(2,1)S(1)}, u32[]{:S(2)}, u32[]{:S(2)}) collective-permute-start(bf16[1792,256]{1,0:T(8,128)(2,1)} %get-tuple-element.31.refs_3_.refs_1_), channel_id=1, source_target_pairs={{0,32},{32,0},{1,33},{33,1},{2,34},{34,2},{3,35},{35,3},{4,36},{36... | collective-permute-start | bytes 2752520 | tf_op jit(solution)/shard_map/ppermute | solution.py:22
  156.9 9.2 %collective-permute-start.19 = (bf16[1792,256]{1,0:T(8,128)(2,1)}, bf16[1792,256]{1,0:T(8,128)(2,1)S(1)}, u32[]{:S(2)}, u32[]{:S(2)}) collective-permute-start(bf16[1792,256]{1,0:T(8,128)(2,1)} %collective-permute-done.17.refs_2_), channel_id=1, source_target_pairs={{0,32},{32,0},{1,33},{33,1},{2,34},{34,2},{3,35},{35,3},{4,36},{36... | collective-permute-start | bytes 2752520 | tf_op jit(solution)/shard_map/ppermute | solution.py:22
  (53 other events, 223.0 us)

commit v4 on v3

--- a/solution.py
+++ b/solution.py
@@ -87,9 +87,8 @@
         copies[k] = total
 
 
-def gather_rows(mine, name, after=()):
+def gather_rows(mine, other, name, after=()):
     count = lax.axis_size(PLANE)
-    other = flip(mine, "xl", 1)
     copies = call(
         spread_kernel, struct(count, *mine.shape, BF), mine, other, name=name, after=after
     )
@@ -213,30 +212,34 @@
             out[here, :] = total.astype(BF)
 
 
+def add_kernel(mine, recv, total):
+    total[...] = mine[...].astype(F32) + recv[...].astype(F32)
+
+
 def assemble_kernel(with_old, core, *refs):
-    mine, recv, mine_o, recv_o = refs[:4]
-    out = refs[4 + with_old]
-
-    def run(a, b, c, d):
-        hc = a.shape[1]
-        out[:, :hc] = a[...].astype(F32) + b[...].astype(F32)
-        out[:, hc:] = c[...].astype(F32) + d[...].astype(F32)
-
-    pl.when(core[0] == 0)(lambda: run(mine, recv, mine_o, recv_o))
-    pl.when(core[0] == 1)(lambda: run(mine_o, recv_o, mine, recv))
-
-
-def assemble(core, four, out, steps, in_start, out_start, old, name):
-    hc = four[0].shape[1]
+    mine, other = refs[:2]
+    out = refs[2 + with_old]
+    hc = mine.shape[1]
+
+    def run(a, b):
+        out[:, :hc] = a[...]
+        out[:, hc:] = b[...]
+
+    pl.when(core[0] == 0)(lambda: run(mine, other))
+    pl.when(core[0] == 1)(lambda: run(other, mine))
+
+
+def assemble(core, two, out, steps, in_start, out_start, old, name):
+    hc = two[0].shape[1]
     bs = out.shape[0]
     half = pl.BlockSpec((bs, hc), lambda k: (k + in_start, 0))
     more = {}
-    specs = [SMEM] + [half] * 4
-    args = [core, *four]
+    specs = [SMEM] + [half] * 2
+    args = [core, *two]
     if old is not None:
         specs.append(pl.BlockSpec(memory_space=pl.ANY))
         args.append(old)
-        more["input_output_aliases"] = {5: 0}
+        more["input_output_aliases"] = {3: 0}
     return call(
         functools.partial(assemble_kernel, old is not None),
         out,
@@ -290,9 +293,9 @@
     )
 
 
-def over_chips(mine):
-    recv = flip(mine, "xh", 1)
-    return mine, recv, flip(mine, "core", 1), flip(recv, "core", 1)
+def over_chips(mine, name, after=()):
+    total = call(add_kernel, struct(*mine.shape, F32), mine, flip(mine, "xh", 1), name="add_" + name, after=after)
+    return total, flip(total, "core", 1)
 
 
 def shards(tokens, butterfly, left_factor, right_factor, cotangent):
@@ -308,7 +311,7 @@
     low_mine = row_sum(scatter_rows(low), "low_sum", (t0, t1a, t3a))
     t1b, t3b = flip(second, "z", 1), flip(second, "y", 1)
     t2a, t4a = flip(t1a, "z", 3), flip(t3a, "y", 3)
-    copies, reduced = gather_rows(low_mine, "low_spread")
+    copies, reduced = gather_rows(low_mine, flip(low_mine, "xl", 1), "low_spread")
     held = hold((t1b, t3b), (copies,), "hold_b")
     t2b, t4b = flip(held[0], "z", 3), flip(held[1], "y", 3)
 
@@ -366,9 +369,9 @@
     )
     g2, g4 = flip(c2, "z", 3), flip(c4, "y", 3)
     back_mine = row_sum(back_pieces, "back_sum", (r0, c2))
-    mine0, mine1 = hold((mine0, mine1), (back_mine,), "hold_halves")
-    four0, four1 = over_chips(mine0), over_chips(mine1)
-    copies, back_reduced = gather_rows(back_mine, "back_spread", (mine0, mine1))
+    back_other = flip(back_mine, "xl", 1)
+    mine0, mine1 = hold((mine0, mine1), (back_other,), "hold_halves")
+    copies, back_reduced = gather_rows(back_mine, back_other, "back_spread", (mine0, mine1))
     s1 = call(
         functools.partial(back_add_kernel, 2),
         full,
@@ -393,7 +396,8 @@
     left_slots = (((0,),),)
     left_got = give_half(core, left_slots, [back_reduced], blocks, "left", (s1, s3), gflop=0.5)
     (mine2,) = keep_half(core, left_got, left_slots, [back_reduced], blocks, "left", gflop=0.5)
-    left_four = over_chips(mine2)
+    left_four = over_chips(mine2, "left")
+    four0, four1 = over_chips(mine0, "0", (mine2,)), over_chips(mine1, "1", (mine2,))
 
     grads = struct(*butterfly.shape, F32)
     grads_a = assemble(core, four0, grads, 3, 0, 0, None, "put0")
@@ -402,7 +406,7 @@
     grad_left = assemble(core, left_four, struct(bs, rank, F32), 1, 0, 0, None, "put_left")
 
     grad_tokens = call(
-        finish_kernel, full, *deltas, butterfly, back_reduced, left_factor, r0, r1, r3, name="finish"
+        finish_kernel, full, *deltas, butterfly, back_reduced, left_factor, r0, r1, r3, name="finish", gflop=15.0
     )
     return (output, grad_tokens, grad_butterfly, grad_left, grad_right)
 

time: 183 us -> 172 us (0.940)
  local copies, waits for them, and re-layouts: 31.7 us -> 20 us
  starting transfers between devices: 64.4 us -> 66.4 us
  waiting for transfers between devices: 30.5 us -> 32.5 us
    unnamed x92 -> x66, local copies, waits for them, and re-layouts: 31.7 us -> 20 us
    ppermute x27 -> x24, starting transfers between devices: 42.2 us -> 44.7 us  [flip(): return lax.ppermute(block, axis, [(i, i ^ mask) for i in range(count)])]
    pallas_call x24 -> x27, Pallas kernels: 51.2 us -> 49.6 us  [call(): pl.pallas_call(body, out_shape=outs, name=name, in_specs=specs + [ANY] *...]
    ppermute x27 -> x24, waiting for transfers between devices: 20.2 us -> 19.9 us  [flip(): return lax.ppermute(block, axis, [(i, i ^ mask) for i in range(count)])]
  transfers between devices with their start and end apart: 31 -> 28, of which waited for: 11 -> 10; matrix products, arithmetic and copies ran while one was open for 1% -> 1% of each run, Pallas kernels for 20% -> 21%
where the time goes in v4:
time: 172 us; the launch traced here: 170 us
  starting transfers between devices  66.4 us (39%)
  Pallas kernels  49.6 us (29%)
  waiting for transfers between devices  32.5 us (19%)
  local copies, waits for them, and re-layouts  20 us (12%)
    pallas_call x27, Pallas kernels, call(): pl.pallas_call(body, out_shape=outs, name=name, in_specs=specs + [ANY] *...  49.6 us
    ppermute x24, starting transfers between devices, flip(): return lax.ppermute(block, axis, [(i, i ^ mask) for i in range(count)])  44.7 us
    unnamed x66, local copies, waits for them, and re-layouts  20 us
    ppermute x24, waiting for transfers between devices, flip(): return lax.ppermute(block, axis, [(i, i ^ mask) for i in range(count)])  19.9 us
    all_to_all x2, starting transfers between devices, scatter_rows(): return lax.all_to_all(part.reshape(count, -1, part.shape[1]), PLANE, 0, 0)  11.9 us
    all_to_all x2, starting transfers between devices, gather_rows(): lax.all_to_all(copies, PLANE, 0, 0).reshape(-1, mine.shape[1])  9.84 us
    all_to_all x2, waiting for transfers between devices, scatter_rows(): return lax.all_to_all(part.reshape(count, -1, part.shape[1]), PLANE, 0, 0)  9.11 us
    all_to_all x2, waiting for transfers between devices, gather_rows(): lax.all_to_all(copies, PLANE, 0, 0).reshape(-1, mine.shape[1])  3.51 us
  transfers between devices with their start and end apart: 28, of which 10 were waited for; matrix products, arithmetic and copies ran while one was open for 1% of the time, Pallas kernels for 21%

profile of v4, /device:TPU:1, one launch (start us, length us, event | category | flops | bytes accessed | tf_op | source)
XLA Modules:
  0.0 170.5 jit_solution(9864405844391877249)
XLA Ops:
  10.0 7.0 %all-to-all-start = ((bf16[16,64,256]{2,1,0:T(8,128)(2,1)}), bf16[16,64,256]{2,1,0:T(8,128)(2,1)S(1)}, u32[]{:S(2)}, u32[]{:S(2)}) async-start(bf16[16,64,256]{2,1,0:T(8,128)(2,1)} %bitcast), calls=%async_computation | async-start | bytes 1048576 | tf_op jit(solution)/shard_map/all_to_all | solution.py:100
  19.6 8.6 %all-to-all-done.refs_0_ = bf16[16,64,256]{2,1,0:T(8,128)(2,1)S(1)} async-done(((bf16[16,64,256]{2,1,0:T(8,128)(2,1)}), bf16[16,64,256]{2,1,0:T(8,128)(2,1)S(1)}, u32[]{:S(2)}, u32[]{:S(2)}) %all-to-all-start) | async-done | bytes 524320 | tf_op jit(solution)/shard_map/all_to_all | solution.py:100
  31.0 2.7 %collective-permute-start.5 = (bf16[512,512]{1,0:T(8,128)(2,1)}, bf16[512,512]{1,0:T(8,128)(2,1)}, u32[]{:S(2)}, u32[]{:S(2)}) collective-permute-start(bf16[512,512]{1,0:T(8,128)(2,1)} %collective-permute-done.2.refs_3_.refs_8_.refs_9_.refs_10_), channel_id=1, source_target_pairs={{0,24},{8,16},{16,8},{24,0},{1,25},{9,17},{17,9},{25,1},{2,26},{10... | collective-permute-start | bytes 1572872 | tf_op jit(solution)/shard_map/ppermute | solution.py:22
  34.6 3.6 %all-to-all-start.1 = ((bf16[16,64,256]{2,1,0:T(8,128)(2,1)}), bf16[16,64,256]{2,1,0:T(8,128)(2,1)S(1)}, u32[]{:S(2)}, u32[]{:S(2)}) async-start(bf16[16,64,256]{2,1,0:T(8,128)(2,1)} %low_spread.1.refs_2_), calls=%async_computation.1 | async-start | bytes 1048576 | tf_op jit(solution)/shard_map/all_to_all | solution.py:95
  40.4 2.6 %collective-permute-start.8 = (bf16[512,512]{1,0:T(8,128)(2,1)}, bf16[512,512]{1,0:T(8,128)(2,1)}, u32[]{:S(2)}, u32[]{:S(2)}) collective-permute-start(bf16[512,512]{1,0:T(8,128)(2,1)} %get-tuple-element.22), channel_id=1, source_target_pairs={{0,6},{2,4},{4,2},{6,0},{1,7},{3,5},{5,3},{7,1},{8,14},{10,12},{12... | collective-permute-start | bytes 1572872 | tf_op jit(solution)/shard_map/ppermute | solution.py:22
  45.4 3.5 %all-to-all-done.1 = bf16[16,64,256]{2,1,0:T(8,128)(2,1)S(1)} async-done(((bf16[16,64,256]{2,1,0:T(8,128)(2,1)}), bf16[16,64,256]{2,1,0:T(8,128)(2,1)S(1)}, u32[]{:S(2)}, u32[]{:S(2)}) %all-to-all-start.1) | async-done | bytes 524320 | tf_op jit(solution)/shard_map/all_to_all | solution.py:95
  52.2 3.9 %forward_a.1 = (bf16[512,512]{1,0:T(8,128)(2,1)S(1)}, bf16[512,512]{1,0:T(8,128)(2,1)S(1)}) custom-call(bf16[1024,256]{1,0:T(8,128)(2,1)S(1)} %bitcast.6, bf16[256,512]{1,0:T(8,128)(2,1)S(1)} %copy-done.29, bf16[1024,512]{1,0:T(8,128)(2,1)S(1)} %copy-done.30, bf16[512,3072]{1,0:T(8,128)(2,1)S(1)} %copy-done.2, bf16[1024,512]{1,0:T(8,128)(2,1)S(1)} %copy-done.1, ...), custom_call_target="tpu_custom_call" | custom-call | flops 4500000768 | bytes 1000 | tf_op jit(solution)/shard_map/forward_a/pallas_call | solution.py:46
  56.2 3.8 %collective-permute-done.8.refs_7_.refs_8_.refs_9_ = bf16[512,512]{1,0:T(8,128)(2,1)} collective-permute-done((bf16[512,512]{1,0:T(8,128)(2,1)}, bf16[512,512]{1,0:T(8,128)(2,1)}, u32[]{:S(2)}, u32[]{:S(2)}) %collective-permute-start.8) | collective-permute-done | bytes 524320 | tf_op jit(solution)/shard_map/ppermute | solution.py:22
  61.4 3.8 %forward_b.1 = (bf16[512,512]{1,0:T(8,128)(2,1)S(1)}, bf16[512,512]{1,0:T(8,128)(2,1)S(1)}) custom-call(bf16[1024,256]{1,0:T(8,128)(2,1)S(1)} %bitcast.7, bf16[256,512]{1,0:T(8,128)(2,1)S(1)} %copy-done.29, bf16[1024,512]{1,0:T(8,128)(2,1)S(1)} %copy-done.31, bf16[512,3072]{1,0:T(8,128)(2,1)S(1)} %copy-done.2, bf16[1024,512]{1,0:T(8,128)(2,1)S(1)} %copy-done.1, ...), custom_call_target="tpu_custom_call" | custom-call | flops 4500000768 | bytes 1000 | tf_op jit(solution)/shard_map/forward_b/pallas_call | solution.py:46
  67.4 5.3 %give_all.1 = bf16[3328,256]{1,0:T(8,128)(2,1)} custom-call(s32[1]{0:T(128)} %bitcast.3.refs_0_, bf16[512,512]{1,0:T(8,128)(2,1)S(1)} %get-tuple-element.24.refs_10_.refs_0_.refs_1_.refs_2_, bf16[512,512]{1,0:T(8,128)(2,1)S(1)} %get-tuple-element.26.refs_1_.refs_2_.refs_3_, bf16[1024,512]{1,0:T(8,128)(2,1)S(1)} %copy-done.1, ...), custom_call_target="tpu_custom_call" | custom-call | flops 4500000768 | bytes 1000 | tf_op jit(solution)/shard_map/give_all/pallas_call | solution.py:46
  72.7 3.8 %collective-permute-start.11 = (bf16[3328,256]{1,0:T(8,128)(2,1)}, bf16[3328,256]{1,0:T(8,128)(2,1)}, u32[]{:S(2)}, u32[]{:S(2)}) collective-permute-start(bf16[3328,256]{1,0:T(8,128)(2,1)} %give_all.1), channel_id=1, source_target_pairs={{0,32},{32,0},{1,33},{33,1},{2,34},{34,2},{3,35},{35,3},{4,36},{36... | collective-permute-start | bytes 5111816 | tf_op jit(solution)/shard_map/ppermute | solution.py:22
  76.5 4.8 %all-to-all-start.2 = ((bf16[16,64,256]{2,1,0:T(8,128)(2,1)}), bf16[16,64,256]{2,1,0:T(8,128)(2,1)}, u32[]{:S(2)}, u32[]{:S(2)}) async-start(bf16[16,64,256]{2,1,0:T(8,128)(2,1)} %bitcast.5), calls=%async_computation.2 | async-start | bytes 1048576 | tf_op jit(solution)/shard_map/all_to_all | solution.py:100
  84.6 4.7 %keep_all.1 = (bf16[1536,256]{1,0:T(8,128)(2,1)S(1)}, bf16[1792,256]{1,0:T(8,128)(2,1)S(1)}) custom-call(s32[1]{0:T(128)} %bitcast.3.refs_0_, bf16[3328,256]{1,0:T(8,128)(2,1)} %collective-permute-done.11.refs_1_, bf16[512,512]{1,0:T(8,128)(2,1)S(1)} %get-tuple-element.24.refs_10_.refs_0_.refs_1_.refs_2_, ...), custom_call_target="tpu_custom_call" | custom-call | flops 4500000768 | bytes 1000 | tf_op jit(solution)/shard_map/keep_all/pallas_call | solution.py:46
  94.6 2.5 %back_far.1 = (bf16[1024,512]{1,0:T(8,128)(2,1)}, bf16[1024,512]{1,0:T(8,128)(2,1)}) custom-call(bf16[512,512]{1,0:T(8,128)(2,1)S(1)} %get-tuple-element.24.refs_10_.refs_0_.refs_1_.refs_2_, bf16[512,512]{1,0:T(8,128)(2,1)S(1)} %get-tuple-element.26.refs_1_.refs_2_.refs_3_, bf16[512,3072]{1,0:T(8,128)(2,1)S(1)} %copy-done.3, ...), custom_call_target="tpu_custom_call" | custom-call | flops 2000001024 | bytes 1000 | tf_op jit(solution)/shard_map/back_far/pallas_call | solution.py:46
  101.4 4.6 %collective-permute-done.10.refs_1_.refs_5_ = bf16[1024,512]{1,0:T(8,128)(2,1)} collective-permute-done((bf16[1024,512]{1,0:T(8,128)(2,1)S(1)}, bf16[1024,512]{1,0:T(8,128)(2,1)}, u32[]{:S(2)}, u32[]{:S(2)}) %collective-permute-start.10) | collective-permute-done | bytes 1048608 | tf_op jit(solution)/shard_map/ppermute | solution.py:22
  108.1 2.6 %collective-permute-done.12.refs_2_.refs_1_ = f32[64,256]{1,0:T(8,128)S(1)} collective-permute-done((f32[64,256]{1,0:T(8,128)S(1)}, f32[64,256]{1,0:T(8,128)S(1)}, u32[]{:S(2)}, u32[]{:S(2)}) %collective-permute-start.12) | collective-permute-done | bytes 65568 | tf_op jit(solution)/shard_map/ppermute | solution.py:22
  110.8 2.5 %collective-permute-start.17 = (bf16[1792,256]{1,0:T(8,128)(2,1)S(1)}, bf16[1792,256]{1,0:T(8,128)(2,1)}, u32[]{:S(2)}, u32[]{:S(2)}) collective-permute-start(bf16[1792,256]{1,0:T(8,128)(2,1)S(1)} %get-tuple-element.31.refs_3_.refs_0_), channel_id=1, source_target_pairs={{0,64},{64,0},{1,65},{65,1},{2,66},{66,2},{3,67},{67,3},{4,68},{68... | collective-permute-start | bytes 2752520 | tf_op jit(solution)/shard_map/ppermute | solution.py:22
  114.2 6.3 %all-to-all-start.3 = ((bf16[16,64,256]{2,1,0:T(8,128)(2,1)}), bf16[16,64,256]{2,1,0:T(8,128)(2,1)}, u32[]{:S(2)}, u32[]{:S(2)}) async-start(bf16[16,64,256]{2,1,0:T(8,128)(2,1)} %copy-done.10), calls=%async_computation.3 | async-start | bytes 1048576 | tf_op jit(solution)/shard_map/all_to_all | solution.py:95
  124.9 2.9 %back_z.1.refs_3_ = bf16[1024,512]{1,0:T(8,128)(2,1)} custom-call(bf16[512,512]{1,0:T(8,128)(2,1)S(1)} %get-tuple-element.24.refs_10_.refs_0_.refs_1_.refs_2_, bf16[512,512]{1,0:T(8,128)(2,1)S(1)} %copy-done.7, bf16[512,3072]{1,0:T(8,128)(2,1)S(1)} %copy-done.4, bf16[1024,512]{1,0:T(8,128)(2,1)} %collective-permute-done.13.refs_3_, ...), custom_call_target="tpu_custom_call" | custom-call | flops 2000001024 | bytes 1000 | tf_op jit(solution)/shard_map/back_z/pallas_call | solution.py:46
  128.7 2.9 %back_y.1.refs_4_ = bf16[1024,512]{1,0:T(8,128)(2,1)} custom-call(bf16[512,512]{1,0:T(8,128)(2,1)S(1)} %get-tuple-element.24.refs_10_.refs_0_.refs_1_.refs_2_, bf16[512,512]{1,0:T(8,128)(2,1)S(1)} %copy-done.7, bf16[512,3072]{1,0:T(8,128)(2,1)S(1)} %copy-done.4, bf16[1024,512]{1,0:T(8,128)(2,1)} %collective-permute-done.15.refs_3_, ...), custom_call_target="tpu_custom_call" | custom-call | flops 2000001024 | bytes 1000 | tf_op jit(solution)/shard_map/back_y/pallas_call | solution.py:46
  137.0 5.2 %collective-permute-start.18 = (bf16[512,128]{1,0:T(8,128)(2,1)S(1)}, bf16[512,128]{1,0:T(8,128)(2,1)S(1)}, u32[]{:S(2)}, u32[]{:S(2)}) collective-permute-start(bf16[512,128]{1,0:T(8,128)(2,1)S(1)} %give_left.1), channel_id=1, source_target_pairs={{0,32},{32,0},{1,33},{33,1},{2,34},{34,2},{3,35},{35,3},{4,36},{36... | collective-permute-start | bytes 393224 | tf_op jit(solution)/shard_map/ppermute | solution.py:22
  146.6 7.2 %collective-permute-done.22.refs_1_ = bf16[512,128]{1,0:T(8,128)(2,1)S(1)} collective-permute-done((bf16[512,128]{1,0:T(8,128)(2,1)S(1)}, bf16[512,128]{1,0:T(8,128)(2,1)S(1)}, u32[]{:S(2)}, u32[]{:S(2)}) %collective-permute-start.22) | collective-permute-done | bytes 131104 | tf_op jit(solution)/shard_map/ppermute | solution.py:22
  153.8 3.6 %collective-permute-start.23 = (f32[512,128]{1,0:T(8,128)S(1)}, f32[512,128]{1,0:T(8,128)S(1)}, u32[]{:S(2)}, u32[]{:S(2)}) collective-permute-start(f32[512,128]{1,0:T(8,128)S(1)} %add_left.1.refs_1_), channel_id=1, source_target_pairs={{0,32},{32,0},{1,33},{33,1},{2,34},{34,2},{3,35},{35,3},{4,36},{36... | collective-permute-start | bytes 786440 | tf_op jit(solution)/shard_map/ppermute | solution.py:22
  161.2 4.2 %finish.1 = bf16[1024,512]{1,0:T(8,128)(2,1)} custom-call(bf16[512,512]{1,0:T(8,128)(2,1)S(1)} %get-tuple-element.24.refs_10_.refs_0_.refs_1_.refs_2_, bf16[512,512]{1,0:T(8,128)(2,1)S(1)} %copy-done.8, bf16[512,3072]{1,0:T(8,128)(2,1)S(1)} %copy-done.5, bf16[1024,256]{1,0:T(8,128)(2,1)} %bitcast.4.refs_3_.refs_1_.refs_2_, bf16[512,256]{1,0:T(8,128)(2,1)S(1)} %copy-done.28, ...), custom_call_target="tpu_custom_call" | custom-call | flops 15000000512 | bytes 1000 | tf_op jit(solution)/shard_map/finish/pallas_call | solution.py:46
  (126 shorter events, 66.7 us)
Async XLA Ops:
  0.6 27.6 %collective-permute-start = (bf16[1024,512]{1,0:T(8,128)(2,1)}, bf16[1024,512]{1,0:T(8,128)(2,1)S(1)}, u32[]{:S(2)}, u32[]{:S(2)}) collective-permute-start(bf16[1024,512]{1,0:T(8,128)(2,1)} %refs_3_.7), channel_id=1, source_target_pairs={{0,1},{1,0},{2,3},{3,2},{4,5},{5,4},{6,7},{7,6},{8,9},{9,8},{10,11... | collective-permute-start | bytes 3145736 | tf_op jit(solution)/shard_map/ppermute | solution.py:22
  4.9 23.3 %collective-permute-start.1 = (bf16[512,512]{1,0:T(8,128)(2,1)}, bf16[512,512]{1,0:T(8,128)(2,1)}, u32[]{:S(2)}, u32[]{:S(2)}) collective-permute-start(bf16[512,512]{1,0:T(8,128)(2,1)} %get-tuple-element.19), channel_id=1, source_target_pairs={{0,2},{2,0},{4,6},{6,4},{1,3},{3,1},{5,7},{7,5},{8,10},{10,8},{12,... | collective-permute-start | bytes 1572872 | tf_op jit(solution)/shard_map/ppermute | solution.py:22
  6.5 21.7 %collective-permute-start.2 = (bf16[512,512]{1,0:T(8,128)(2,1)}, bf16[512,512]{1,0:T(8,128)(2,1)}, u32[]{:S(2)}, u32[]{:S(2)}) collective-permute-start(bf16[512,512]{1,0:T(8,128)(2,1)} %get-tuple-element.19), channel_id=1, source_target_pairs={{0,8},{8,0},{16,24},{24,16},{1,9},{9,1},{17,25},{25,17},{2,10},{10... | collective-permute-start | bytes 1572872 | tf_op jit(solution)/shard_map/ppermute | solution.py:22
  10.0 18.2 %all-to-all-start = ((bf16[16,64,256]{2,1,0:T(8,128)(2,1)}), bf16[16,64,256]{2,1,0:T(8,128)(2,1)S(1)}, u32[]{:S(2)}, u32[]{:S(2)}) async-start(bf16[16,64,256]{2,1,0:T(8,128)(2,1)} %bitcast), calls=%async_computation | async-start | bytes 1048576 | tf_op jit(solution)/shard_map/all_to_all | solution.py:100
  17.0 21.2 %collective-permute-start.6 = (bf16[512,512]{1,0:T(8,128)(2,1)}, bf16[512,512]{1,0:T(8,128)(2,1)}, u32[]{:S(2)}, u32[]{:S(2)}) collective-permute-start(bf16[512,512]{1,0:T(8,128)(2,1)} %copy-done.32), channel_id=1, source_target_pairs={{0,2},{2,0},{4,6},{6,4},{1,3},{3,1},{5,7},{7,5},{8,10},{10,8},{12,... | collective-permute-start | bytes 1572872 | tf_op jit(solution)/shard_map/ppermute | solution.py:22
  18.4 19.8 %collective-permute-start.7 = (bf16[512,512]{1,0:T(8,128)(2,1)}, bf16[512,512]{1,0:T(8,128)(2,1)}, u32[]{:S(2)}, u32[]{:S(2)}) collective-permute-start(bf16[512,512]{1,0:T(8,128)(2,1)} %copy-done.32), channel_id=1, source_target_pairs={{0,8},{8,0},{16,24},{24,16},{1,9},{9,1},{17,25},{25,17},{2,10},{10... | collective-permute-start | bytes 1572872 | tf_op jit(solution)/shard_map/ppermute | solution.py:22
  28.7 16.7 %collective-permute-start.4 = (bf16[512,512]{1,0:T(8,128)(2,1)}, bf16[512,512]{1,0:T(8,128)(2,1)}, u32[]{:S(2)}, u32[]{:S(2)}) collective-permute-start(bf16[512,512]{1,0:T(8,128)(2,1)} %collective-permute-done.1.refs_2_.refs_6_.refs_5_), channel_id=1, source_target_pairs={{0,6},{2,4},{4,2},{6,0},{1,7},{3,5},{5,3},{7,1},{8,14},{10,12},{12... | collective-permute-start | bytes 1572872 | tf_op jit(solution)/shard_map/ppermute | solution.py:22
  31.0 14.4 %collective-permute-start.5 = (bf16[512,512]{1,0:T(8,128)(2,1)}, bf16[512,512]{1,0:T(8,128)(2,1)}, u32[]{:S(2)}, u32[]{:S(2)}) collective-permute-start(bf16[512,512]{1,0:T(8,128)(2,1)} %collective-permute-done.2.refs_3_.refs_8_.refs_9_.refs_10_), channel_id=1, source_target_pairs={{0,24},{8,16},{16,8},{24,0},{1,25},{9,17},{17,9},{25,1},{2,26},{10... | collective-permute-start | bytes 1572872 | tf_op jit(solution)/shard_map/ppermute | solution.py:22
  34.6 14.3 %all-to-all-start.1 = ((bf16[16,64,256]{2,1,0:T(8,128)(2,1)}), bf16[16,64,256]{2,1,0:T(8,128)(2,1)S(1)}, u32[]{:S(2)}, u32[]{:S(2)}) async-start(bf16[16,64,256]{2,1,0:T(8,128)(2,1)} %low_spread.1.refs_2_), calls=%async_computation.1 | async-start | bytes 1048576 | tf_op jit(solution)/shard_map/all_to_all | solution.py:95
  40.4 19.6 %collective-permute-start.8 = (bf16[512,512]{1,0:T(8,128)(2,1)}, bf16[512,512]{1,0:T(8,128)(2,1)}, u32[]{:S(2)}, u32[]{:S(2)}) collective-permute-start(bf16[512,512]{1,0:T(8,128)(2,1)} %get-tuple-element.22), channel_id=1, source_target_pairs={{0,6},{2,4},{4,2},{6,0},{1,7},{3,5},{5,3},{7,1},{8,14},{10,12},{12... | collective-permute-start | bytes 1572872 | tf_op jit(solution)/shard_map/ppermute | solution.py:22
  43.0 17.1 %collective-permute-start.9 = (bf16[512,512]{1,0:T(8,128)(2,1)}, bf16[512,512]{1,0:T(8,128)(2,1)}, u32[]{:S(2)}, u32[]{:S(2)}) collective-permute-start(bf16[512,512]{1,0:T(8,128)(2,1)} %get-tuple-element.23), channel_id=1, source_target_pairs={{0,24},{8,16},{16,8},{24,0},{1,25},{9,17},{17,9},{25,1},{2,26},{10... | collective-permute-start | bytes 1572872 | tf_op jit(solution)/shard_map/ppermute | solution.py:22
  72.7 9.7 %collective-permute-start.11 = (bf16[3328,256]{1,0:T(8,128)(2,1)}, bf16[3328,256]{1,0:T(8,128)(2,1)}, u32[]{:S(2)}, u32[]{:S(2)}) collective-permute-start(bf16[3328,256]{1,0:T(8,128)(2,1)} %give_all.1), channel_id=1, source_target_pairs={{0,32},{32,0},{1,33},{33,1},{2,34},{34,2},{3,35},{35,3},{4,36},{36... | collective-permute-start | bytes 5111816 | tf_op jit(solution)/shard_map/ppermute | solution.py:22
  76.5 15.0 %all-to-all-start.2 = ((bf16[16,64,256]{2,1,0:T(8,128)(2,1)}), bf16[16,64,256]{2,1,0:T(8,128)(2,1)}, u32[]{:S(2)}, u32[]{:S(2)}) async-start(bf16[16,64,256]{2,1,0:T(8,128)(2,1)} %bitcast.5), calls=%async_computation.2 | async-start | bytes 1048576 | tf_op jit(solution)/shard_map/all_to_all | solution.py:100
  81.4 24.6 %collective-permute-start.10 = (bf16[1024,512]{1,0:T(8,128)(2,1)S(1)}, bf16[1024,512]{1,0:T(8,128)(2,1)}, u32[]{:S(2)}, u32[]{:S(2)}) collective-permute-start(bf16[1024,512]{1,0:T(8,128)(2,1)S(1)} %back_x.1.refs_3_), channel_id=1, source_target_pairs={{0,1},{1,0},{2,3},{3,2},{4,5},{5,4},{6,7},{7,6},{8,9},{9,8},{10,11... | collective-permute-start | bytes 3145736 | tf_op jit(solution)/shard_map/ppermute | solution.py:22
  97.1 23.9 %collective-permute-start.13 = (bf16[1024,512]{1,0:T(8,128)(2,1)}, bf16[1024,512]{1,0:T(8,128)(2,1)}, u32[]{:S(2)}, u32[]{:S(2)}) collective-permute-start(bf16[1024,512]{1,0:T(8,128)(2,1)} %get-tuple-element.28.refs_2_), channel_id=1, source_target_pairs={{0,6},{2,4},{4,2},{6,0},{1,7},{3,5},{5,3},{7,1},{8,14},{10,12},{12... | collective-permute-start | bytes 3145736 | tf_op jit(solution)/shard_map/ppermute | solution.py:22
  99.0 29.7 %collective-permute-start.15 = (bf16[1024,512]{1,0:T(8,128)(2,1)}, bf16[1024,512]{1,0:T(8,128)(2,1)}, u32[]{:S(2)}, u32[]{:S(2)}) collective-permute-start(bf16[1024,512]{1,0:T(8,128)(2,1)} %get-tuple-element.32), channel_id=1, source_target_pairs={{0,24},{8,16},{16,8},{24,0},{1,25},{9,17},{17,9},{25,1},{2,26},{10... | collective-permute-start | bytes 3145736 | tf_op jit(solution)/shard_map/ppermute | solution.py:22
  110.8 33.9 %collective-permute-start.17 = (bf16[1792,256]{1,0:T(8,128)(2,1)S(1)}, bf16[1792,256]{1,0:T(8,128)(2,1)}, u32[]{:S(2)}, u32[]{:S(2)}) collective-permute-start(bf16[1792,256]{1,0:T(8,128)(2,1)S(1)} %get-tuple-element.31.refs_3_.refs_0_), channel_id=1, source_target_pairs={{0,64},{64,0},{1,65},{65,1},{2,66},{66,2},{3,67},{67,3},{4,68},{68... | collective-permute-start | bytes 2752520 | tf_op jit(solution)/shard_map/ppermute | solution.py:22
  114.2 21.2 %all-to-all-start.3 = ((bf16[16,64,256]{2,1,0:T(8,128)(2,1)}), bf16[16,64,256]{2,1,0:T(8,128)(2,1)}, u32[]{:S(2)}, u32[]{:S(2)}) async-start(bf16[16,64,256]{2,1,0:T(8,128)(2,1)} %copy-done.10), calls=%async_computation.3 | async-start | bytes 1048576 | tf_op jit(solution)/shard_map/all_to_all | solution.py:95
  127.9 32.9 %collective-permute-start.14 = (bf16[1024,512]{1,0:T(8,128)(2,1)}, bf16[1024,512]{1,0:T(8,128)(2,1)}, u32[]{:S(2)}, u32[]{:S(2)}) collective-permute-start(bf16[1024,512]{1,0:T(8,128)(2,1)} %back_z.1.refs_3_), channel_id=1, source_target_pairs={{0,2},{2,0},{4,6},{6,4},{1,3},{3,1},{5,7},{7,5},{8,10},{10,8},{12,... | collective-permute-start | bytes 3145736 | tf_op jit(solution)/shard_map/ppermute | solution.py:22
  131.7 29.1 %collective-permute-start.16 = (bf16[1024,512]{1,0:T(8,128)(2,1)}, bf16[1024,512]{1,0:T(8,128)(2,1)}, u32[]{:S(2)}, u32[]{:S(2)}) collective-permute-start(bf16[1024,512]{1,0:T(8,128)(2,1)} %back_y.1.refs_4_), channel_id=1, source_target_pairs={{0,8},{8,0},{16,24},{24,16},{1,9},{9,1},{17,25},{25,17},{2,10},{10... | collective-permute-start | bytes 3145736 | tf_op jit(solution)/shard_map/ppermute | solution.py:22
  133.0 24.4 %collective-permute-start.20 = (bf16[1536,256]{1,0:T(8,128)(2,1)S(1)}, bf16[1536,256]{1,0:T(8,128)(2,1)}, u32[]{:S(2)}, u32[]{:S(2)}) collective-permute-start(bf16[1536,256]{1,0:T(8,128)(2,1)S(1)} %get-tuple-element.30.refs_2_.refs_0_), channel_id=1, source_target_pairs={{0,64},{64,0},{1,65},{65,1},{2,66},{66,2},{3,67},{67,3},{4,68},{68... | collective-permute-start | bytes 2359304 | tf_op jit(solution)/shard_map/ppermute | solution.py:22
  146.1 21.4 %collective-permute-start.19 = (f32[1792,256]{1,0:T(8,128)S(1)}, f32[1792,256]{1,0:T(8,128)S(1)}, u32[]{:S(2)}, u32[]{:S(2)}) collective-permute-start(f32[1792,256]{1,0:T(8,128)S(1)} %add_1.1.refs_1_), channel_id=1, source_target_pairs={{0,32},{32,0},{1,33},{33,1},{2,34},{34,2},{3,35},{35,3},{4,36},{36... | collective-permute-start | bytes 5505032 | tf_op jit(solution)/shard_map/ppermute | solution.py:22
  146.5 7.2 %collective-permute-start.22 = (bf16[512,128]{1,0:T(8,128)(2,1)S(1)}, bf16[512,128]{1,0:T(8,128)(2,1)S(1)}, u32[]{:S(2)}, u32[]{:S(2)}) collective-permute-start(bf16[512,128]{1,0:T(8,128)(2,1)S(1)} %keep_left.1.refs_2_.refs_0_), channel_id=1, source_target_pairs={{0,64},{64,0},{1,65},{65,1},{2,66},{66,2},{3,67},{67,3},{4,68},{68... | collective-permute-start | bytes 393224 | tf_op jit(solution)/shard_map/ppermute | solution.py:22
  158.7 6.7 %collective-permute-start.21 = (f32[1536,256]{1,0:T(8,128)S(1)}, f32[1536,256]{1,0:T(8,128)S(1)}, u32[]{:S(2)}, u32[]{:S(2)}) collective-permute-start(f32[1536,256]{1,0:T(8,128)S(1)} %add_0.1.refs_1_), channel_id=1, source_target_pairs={{0,32},{32,0},{1,33},{33,1},{2,34},{34,2},{3,35},{35,3},{4,36},{36... | collective-permute-start | bytes 4718600 | tf_op jit(solution)/shard_map/ppermute | solution.py:22
  (37 other events, 216.2 us)
